TPU v7x, 128 devices: a whole 4x4x4 slice. The times are simulated.
128 devices in a mesh: dp: 4 (over z), verts: 32 (over y, x, core).
Axes of the slice: x: 4, y: 4, z: 4, core: 2. Of those that a mesh axis runs over, the one named last changes fastest.
Arguments:
- feats: bfloat16 [4, 32768, 512], P('dp', 'verts'), may hold values from -64 to 64
- weights: bfloat16 [4, 512, 512], replicated, may hold values from -0.25 to 0.25
- grad_out: bfloat16 [4, 32768, 512], P('dp', 'verts'), may hold values from -6 to 6
- neighbours: int32 [512, 8], replicated, may hold values from 0 to 511, as said below
- valid: int32 [512, 64], replicated, may hold values from 0 to 1, as said below
Outputs:
- attn_out: bfloat16 [4, 32768, 512], P('dp', 'verts')
- grad_feats: bfloat16 [4, 32768, 512], P('dp', 'verts')
- grad_weights: float32 [4, 512, 512], P(None, 'dp')
Inputs may be any that keep to these rules, and one draw needn't show every extreme that they name: `neighbours`: entry 0 of block b is b; entries 1 to 3 are other blocks of the same partition of 16 blocks (partition b // 16); entries 4 to 7 lie on four different other partitions. The blocks of one partition name exactly 2 distinct blocks of each other partition. A row names no block twice. `valid`: in each block the real vertices come first and are 32 or more.
All inputs are finite; a program needn't handle non-finite values.
Results may differ from a plain program's by a relative error of at most 0.0095.
The roundings to bfloat16 on the way count: a program that leaves them out, or rounds other values in their place, can miss the bound.
Values may be sent and summed in bfloat16 or wider, within the bound.
No kernel may reach another device: no remote copies, remote signals or barrier semaphores. Data moves between devices by JAX's collectives and lax.ppermute only.
A program may use at most 256 MiB of HBM per device.

v0:
```python
import math

import jax
import jax.numpy as jnp
from jax import lax
from jax.sharding import PartitionSpec as P

H = 8
BS = 64
NNB = 8
CAP = 2


def block_pass(query_blk, grad_blk, key_blk, value_blk, key_ok, scaling):
    scores = (
        jnp.einsum("gqhd,gkhd->ghqk", query_blk, key_blk, preferred_element_type=jnp.float32)
        * scaling
    )
    scores = jnp.where(key_ok[:, None, None, :], scores, -jnp.inf)
    row_top = jnp.max(scores, axis=-1, keepdims=True)
    raised = jnp.exp(scores - row_top)
    probs_f = raised / jnp.sum(raised, axis=-1, keepdims=True)
    probs_b = probs_f.astype(jnp.bfloat16)
    attended = jnp.einsum(
        "ghqk,gkhd->gqhd", probs_b, value_blk, preferred_element_type=jnp.float32
    ).astype(jnp.bfloat16)
    dprob = jnp.einsum("gqhd,gkhd->ghqk", grad_blk, value_blk, preferred_element_type=jnp.float32)
    inner_sum = jnp.sum(probs_f * dprob, axis=-1, keepdims=True)
    dscore = (probs_f * (dprob - inner_sum) * scaling).astype(jnp.bfloat16)
    grad_q = jnp.einsum(
        "ghqk,gkhd->gqhd", dscore, key_blk, preferred_element_type=jnp.float32
    ).astype(jnp.bfloat16)
    grad_keys = jnp.einsum("ghqk,gqhd->gkhd", dscore, query_blk, preferred_element_type=jnp.float32)
    grad_values = jnp.einsum(
        "ghqk,gqhd->gkhd", probs_b, grad_blk, preferred_element_type=jnp.float32
    )
    return (attended, grad_q, grad_keys, grad_values)


def local(feats, weights, grad_out, neighbours, valid):
    nparts = lax.axis_size("verts")
    my_index = lax.axis_index("verts")
    subjects_here, rows_here, feature_dim = feats.shape
    blocks = rows_here // BS
    head_dim = feature_dim // H
    scaling = 1.0 / math.sqrt(head_dim)
    all_blocks = neighbours.shape[0]
    first_block = my_index * blocks
    block_ids = jnp.arange(blocks, dtype=jnp.int32)
    slot_ids = jnp.arange(CAP, dtype=jnp.int32)
    global_ids = jnp.arange(all_blocks, dtype=jnp.int32)
    part_ids = jnp.arange(nparts, dtype=jnp.int32)
    my_lists = lax.dynamic_slice_in_dim(neighbours, first_block, blocks, 0)
    flat_ids = my_lists.reshape(-1)
    hit_table = flat_ids[:, None] == global_ids[None, :]
    need_glob = jnp.any(hit_table, axis=0) & (global_ids // blocks != my_index)
    need_grid = need_glob.reshape(nparts, blocks).astype(jnp.int32)
    slot_grid = jnp.cumsum(need_grid, axis=1) - 1
    pick_recv = (need_grid[:, None, :] == 1) & (slot_grid[:, None, :] == slot_ids[None, :, None])
    recv_local = jnp.sum(jnp.where(pick_recv, block_ids[None, None, :], 0), axis=2)
    recv_gid = part_ids[:, None] * blocks + recv_local
    slot_flat = jnp.sum(jnp.where(hit_table, slot_grid.reshape(-1)[None, :], 0), axis=1)
    owner_flat = flat_ids // blocks
    entries = jnp.where(
        owner_flat == my_index, flat_ids - first_block, blocks + owner_flat * CAP + slot_flat
    )
    entries = entries.reshape(blocks // 8, 8, NNB)
    asked = jnp.any(
        neighbours.reshape(nparts, blocks * NNB)[:, :, None]
        == (first_block + block_ids)[None, None, :],
        axis=1,
    )
    asked = (asked & (part_ids[:, None] != my_index)).astype(jnp.int32)
    asked_slot = jnp.cumsum(asked, axis=1) - 1
    pick_send = (asked[:, None, :] == 1) & (asked_slot[:, None, :] == slot_ids[None, :, None])
    send_local = jnp.sum(jnp.where(pick_send, block_ids[None, None, :], 0), axis=2)
    pick_send_f = pick_send.astype(jnp.float32)
    table_gid = jnp.concatenate([first_block + block_ids, recv_gid.reshape(-1)])
    table_ok = jnp.take(valid, table_gid, axis=0) > 0
    w_kv = jnp.concatenate([weights[1], weights[2]], axis=1)
    inputs_now = feats[0]
    cotangent = grad_out[0]
    queries = jnp.dot(inputs_now, weights[0], preferred_element_type=jnp.float32).astype(
        jnp.bfloat16
    )
    key_vals = jnp.dot(inputs_now, w_kv, preferred_element_type=jnp.float32).astype(jnp.bfloat16)
    kv_blocks = key_vals.reshape(blocks, BS, 2 * feature_dim)
    outgoing = kv_blocks[send_local]
    incoming = lax.all_to_all(outgoing, "verts", split_axis=0, concat_axis=0, tiled=True)
    table_kv = jnp.concatenate(
        [kv_blocks, incoming.reshape(nparts * CAP, BS, 2 * feature_dim)], axis=0
    )
    upstream = jnp.dot(cotangent, weights[3].T, preferred_element_type=jnp.float32).astype(
        jnp.bfloat16
    )
    query_groups = queries.reshape(blocks // 8, 8, BS, H, head_dim)
    grad_groups = upstream.reshape(blocks // 8, 8, BS, H, head_dim)

    def group_step(totals, inputs):
        query_blk, grad_blk, group_entries = inputs
        entry_ids = group_entries.reshape(-1)
        fetched = table_kv[entry_ids].reshape(8, NNB * BS, 2, H, head_dim)
        key_ok = table_ok[entry_ids].reshape(8, NNB * BS)
        attended, grad_q, grad_keys, grad_values = block_pass(
            query_blk, grad_blk, fetched[:, :, 0], fetched[:, :, 1], key_ok, scaling
        )
        both_grads = jnp.stack([grad_keys, grad_values], axis=2).reshape(
            8 * NNB, BS, 2 * feature_dim
        )
        return (totals.at[entry_ids].add(both_grads), (attended, grad_q))

    start_tot = jnp.zeros((blocks + nparts * CAP, BS, 2 * feature_dim), jnp.float32)
    totals, (attended, grad_q) = lax.scan(
        group_step, start_tot, (query_groups, grad_groups, entries)
    )
    remote_part = totals[blocks:].reshape(nparts, CAP, BS, 2 * feature_dim)
    returned = lax.all_to_all(remote_part, "verts", split_axis=0, concat_axis=0, tiled=True)
    gathered_back = jnp.einsum(
        "pcj,pcbe->jbe", pick_send_f, returned, precision=lax.Precision.HIGHEST
    )
    grad_kv = (
        (totals[:blocks] + gathered_back).reshape(rows_here, 2 * feature_dim).astype(jnp.bfloat16)
    )
    attended = attended.reshape(rows_here, feature_dim)
    grad_q = grad_q.reshape(rows_here, feature_dim)
    outputs = [
        jnp.dot(attended, weights[3], preferred_element_type=jnp.float32).astype(jnp.bfloat16)
    ]
    grad_sum = jnp.dot(grad_q, weights[0].T, preferred_element_type=jnp.float32) + jnp.dot(
        grad_kv, w_kv.T, preferred_element_type=jnp.float32
    )
    grads_in = [grad_sum.astype(jnp.bfloat16)]
    grad_wkv = jnp.dot(inputs_now.T, grad_kv, preferred_element_type=jnp.float32)
    terms = jnp.stack(
        [
            jnp.dot(inputs_now.T, grad_q, preferred_element_type=jnp.float32),
            grad_wkv[:, :feature_dim],
            grad_wkv[:, feature_dim:],
            jnp.dot(attended.T, cotangent, preferred_element_type=jnp.float32),
        ]
    )
    summed_verts = lax.psum(terms, "verts")
    grad_weights = lax.psum_scatter(summed_verts, "dp", scatter_dimension=1, tiled=True)
    return (jnp.stack(outputs), jnp.stack(grads_in), grad_weights)


def solution(mesh):
    in_specs = (P("dp", "verts", None), P(), P("dp", "verts", None), P(), P())
    out_specs = (P("dp", "verts", None), P("dp", "verts", None), P(None, "dp", None))
    return jax.shard_map(local, mesh=mesh, in_specs=in_specs, out_specs=out_specs, check_vma=False)
```

profile of v0, /device:TPU:1, one launch (start us, length us, event | category | flops | bytes accessed | tf_op | source)
XLA Modules:
  0.0 1109.9 jit_solution(11016948038938764968)
XLA Ops:
  13.0 5.6 gather_fusion.3
  18.6 8.7 all-to-all-start
  34.0 3.9 reshape.293
  40.7 3.9 reshape.290
  45.5 81.6 %all-to-all-done = bf16[32,2,64,1024]{3,2,1,0:T(8,128)(2,1)} async-done(((bf16[32,2,64,1024]{3,2,1,0:T(8,128)(2,1)}), bf16[32,2,64,1024]{3,2,1,0:T(8,128)(2,1)}, u32[]{:S(2)}, u32[]{:S(2)}) %all-to-all-start) | async-done | bytes 8388640 | tf_op jit(solution)/shard_map/all_to_all | solution.py:89
  127.1 8.6 pad_maximum_fusion.1
  135.7 9.7 broadcast_in_dim.83
  145.4 529.7 %while.14 = (s32[]{:T(128)}, f32[80,64,1024]{2,1,0:T(8,128)}, bf16[2,8,64,8,64]{4,3,2,1,0:T(8,128)(2,1)}, bf16[2,8,64,8,64]{4,3,2,1,0:T(8,128)(2,1)}, s32[2,8,8]...) while((s32[]{:T(128)}, f32[80,64,1024]{2,1,0:T(8,128)}, ...), condition=%wide.region_12.13_spmd, body=%wide.region_7.12_spmd.sunk | while | flops 1669868288 | bytes 415345920 | solution.py:113
  149.1 9.6 gather_fusion
  158.7 22.1 %reshape.356 = bf16[8,512,2,8,64]{4,3,2,1,0:T(8,128)(2,1)} reshape(bf16[64,64,1024]{2,1,0:T(8,128)(2,1)} %gather_fusion) | data formatting | bytes 16777216 | tf_op jit(solution)/shard_map/while/body/eval_jaxpr/reshape | solution.py:102
  180.8 11.4 %fusion.127 = (bf16[8,512,1,8,64]{4,3,2,1,0:T(8,128)(2,1)}, bf16[8,512,1,8,64]{4,3,2,1,0:T(8,128)(2,1)}) fusion(bf16[8,512,2,8,64]{4,3,2,1,0:T(8,128)(2,1)} %reshape.356), kind=kLoop, calls=%fused_computation.138.clone.1 | loop fusion | bytes 16777216 | tf_op jit(solution)/shard_map/while/body/eval_jaxpr/slice | solution.py:105
  192.2 9.7 copy.140
  201.9 9.8 copy.141
  211.7 6.9 fusion.130
  219.8 4.7 fusion.129
  224.5 5.7 fusion.133
  230.2 35.3 %fusion.132 = bf16[1,8,64,8,64]{2,4,3,1,0:T(8,128)(2,1)} fusion(f32[8,8,64,512]{3,2,1,0:T(8,128)} %fusion.130, bf16[8,512,1,8,64]{1,4,3,0,2:T(8,128)(2,1)} %copy.140, f32[8,8,64,512]{3,2,1,0:T(8,128)} %get-tuple-element.197, f32[8,8,64]{2,1,0:T(8,128)S(1)} %get-tuple-element.198), kind=kOutput, calls=%fused_computation.34.clone.1 | convolution fusion | flops 283382272 | bytes 21512192 | tf_op jit(solution)/shard_map/while/body/eval_jaxpr/ghqk,gkhd->gqhd/dot_general | solution.py:30
  265.5 35.5 %fusion.131 = f32[8,512,1,8,64]{1,4,3,0,2:T(8,128)} fusion(f32[8,8,64,512]{3,2,1,0:T(8,128)} %fusion.130, bf16[1,8,64,8,64]{4,3,2,1,0:T(8,128)(2,1)S(1)} %constant_dynamic-slice_fusion.9, f32[8,8,64,512]{3,2,1,0:T(8,128)} %get-tuple-element.197, f32[8,8,64]{2,1,0:T(8,128)S(1)} %get-tuple-element.198), kind=kOutput, calls=%fused_computation.28.clone.1 | convolution fusion | flops 283120128 | bytes 25706496 | tf_op jit(solution)/shard_map/while/body/eval_jaxpr/ghqk,gqhd->gkhd/dot_general | solution.py:33
  301.0 4.5 convolution_bitcast_fusion.5
  306.8 6.2 pad_maximum_fusion.7
  317.0 27.6 %copy.142 = f32[8,512,2,8,64]{4,3,2,1,0:T(8,128)} copy(f32[8,512,2,8,64]{1,4,3,0,2:T(8,128)} %pad_maximum_fusion.7) | data formatting | bytes 33554432 | tf_op jit(solution)/shard_map/while/body/eval_jaxpr/stack | solution.py:107
  344.5 28.3 %reshape.357 = f32[64,64,1024]{2,1,0:T(8,128)} reshape(f32[8,512,2,8,64]{4,3,2,1,0:T(8,128)} %copy.142) | data formatting | bytes 33554432 | tf_op jit(solution)/shard_map/while/body/eval_jaxpr/reshape | solution.py:107
  372.8 37.2 %scatter_fusion = f32[80,64,1024]{2,1,0:T(8,128)} fusion(f32[80,64,1024]{2,1,0:T(8,128)} %get-tuple-element.213, s32[64]{0:T(128)S(1)} %fusion.126, f32[64,64,1024]{2,1,0:T(8,128)} %reshape.357), kind=kCustom, calls=%fused_computation.4.clone.1 | custom fusion | flops 4194304 | bytes 50331904 | tf_op jit(solution)/shard_map/while/body/eval_jaxpr/scatter-add | solution.py:110
  413.6 9.6 gather_fusion
  423.1 22.1 %reshape.356 = bf16[8,512,2,8,64]{4,3,2,1,0:T(8,128)(2,1)} reshape(bf16[64,64,1024]{2,1,0:T(8,128)(2,1)} %gather_fusion) | data formatting | bytes 16777216 | tf_op jit(solution)/shard_map/while/body/eval_jaxpr/reshape | solution.py:102
  445.3 11.4 %fusion.127 = (bf16[8,512,1,8,64]{4,3,2,1,0:T(8,128)(2,1)}, bf16[8,512,1,8,64]{4,3,2,1,0:T(8,128)(2,1)}) fusion(bf16[8,512,2,8,64]{4,3,2,1,0:T(8,128)(2,1)} %reshape.356), kind=kLoop, calls=%fused_computation.138.clone.1 | loop fusion | bytes 16777216 | tf_op jit(solution)/shard_map/while/body/eval_jaxpr/slice | solution.py:105
  456.7 9.7 copy.140
  466.4 9.8 copy.141
  476.2 6.9 fusion.130
  484.3 4.7 fusion.129
  489.0 5.7 fusion.133
  494.7 35.3 %fusion.132 = bf16[1,8,64,8,64]{2,4,3,1,0:T(8,128)(2,1)} fusion(f32[8,8,64,512]{3,2,1,0:T(8,128)} %fusion.130, bf16[8,512,1,8,64]{1,4,3,0,2:T(8,128)(2,1)} %copy.140, f32[8,8,64,512]{3,2,1,0:T(8,128)} %get-tuple-element.197, f32[8,8,64]{2,1,0:T(8,128)S(1)} %get-tuple-element.198), kind=kOutput, calls=%fused_computation.34.clone.1 | convolution fusion | flops 283382272 | bytes 21512192 | tf_op jit(solution)/shard_map/while/body/eval_jaxpr/ghqk,gkhd->gqhd/dot_general | solution.py:30
  529.9 35.5 %fusion.131 = f32[8,512,1,8,64]{1,4,3,0,2:T(8,128)} fusion(f32[8,8,64,512]{3,2,1,0:T(8,128)} %fusion.130, bf16[1,8,64,8,64]{4,3,2,1,0:T(8,128)(2,1)S(1)} %constant_dynamic-slice_fusion.9, f32[8,8,64,512]{3,2,1,0:T(8,128)} %get-tuple-element.197, f32[8,8,64]{2,1,0:T(8,128)S(1)} %get-tuple-element.198), kind=kOutput, calls=%fused_computation.28.clone.1 | convolution fusion | flops 283120128 | bytes 25706496 | tf_op jit(solution)/shard_map/while/body/eval_jaxpr/ghqk,gqhd->gkhd/dot_general | solution.py:33
  565.4 4.5 convolution_bitcast_fusion.5
  571.3 6.2 pad_maximum_fusion.7
  581.4 27.6 %copy.142 = f32[8,512,2,8,64]{4,3,2,1,0:T(8,128)} copy(f32[8,512,2,8,64]{1,4,3,0,2:T(8,128)} %pad_maximum_fusion.7) | data formatting | bytes 33554432 | tf_op jit(solution)/shard_map/while/body/eval_jaxpr/stack | solution.py:107
  608.9 28.3 %reshape.357 = f32[64,64,1024]{2,1,0:T(8,128)} reshape(f32[8,512,2,8,64]{4,3,2,1,0:T(8,128)} %copy.142) | data formatting | bytes 33554432 | tf_op jit(solution)/shard_map/while/body/eval_jaxpr/reshape | solution.py:107
  637.3 37.5 %scatter_fusion = f32[80,64,1024]{2,1,0:T(8,128)} fusion(f32[80,64,1024]{2,1,0:T(8,128)} %get-tuple-element.213, s32[64]{0:T(128)S(1)} %fusion.126, f32[64,64,1024]{2,1,0:T(8,128)} %reshape.357), kind=kCustom, calls=%fused_computation.4.clone.1 | custom fusion | flops 4194304 | bytes 50331904 | tf_op jit(solution)/shard_map/while/body/eval_jaxpr/scatter-add | solution.py:110
  675.1 6.6 slice.37
  681.7 14.4 %copy.97 = f32[32,2,64,1024]{3,1,2,0:T(2,128)} copy(f32[32,2,64,1024]{3,2,1,0:T(8,128)S(1)} %bitcast.149) | data formatting | bytes 33554432 | tf_op jit(solution)/shard_map/reshape | solution.py:116
  696.1 11.3 %all-to-all-start.1 = ((f32[32,2,64,1024]{3,1,2,0:T(2,128)}), f32[32,2,64,1024]{3,1,2,0:T(2,128)}, u32[]{:S(2)}, u32[]{:S(2)}) async-start(f32[32,2,64,1024]{3,1,2,0:T(2,128)} %copy.97), calls=%async_computation.1 | async-start | bytes 33554432 | tf_op jit(solution)/shard_map/all_to_all | solution.py:117
  707.4 21.3 %copy.96 = f32[80,64,1024]{2,0,1:T(8,128)} copy(f32[80,64,1024]{2,1,0:T(8,128)} %get-tuple-element.54) | data formatting | bytes 41943040 | tf_op jit(solution)/shard_map/while | solution.py:113
  728.7 3.2 reshape.295
  732.0 3.2 reshape.294
  739.8 169.1 %all-to-all-done.1 = f32[32,2,64,1024]{3,1,2,0:T(2,128)} async-done(((f32[32,2,64,1024]{3,1,2,0:T(2,128)}), f32[32,2,64,1024]{3,1,2,0:T(2,128)}, u32[]{:S(2)}, u32[]{:S(2)}) %all-to-all-start.1) | async-done | bytes 16777248 | tf_op jit(solution)/shard_map/all_to_all | solution.py:117
  908.9 20.9 %fusion.56 = bf16[16,64,1024]{2,0,1:T(8,128)(2,1)S(1)} fusion(f32[80,64,1024]{2,0,1:T(8,128)} %copy.96, f32[32,2,64,1024]{3,1,2,0:T(2,128)} %all-to-all-done.1, s32[32,16]{0,1:T(8,128)S(1)} %copy-done.12, pred[32,16]{0,1:T(8,128)(4,1)S(1)} %copy-done.14), kind=kOutput, calls=%fused_computation.55 | convolution fusion | flops 807405568 | bytes 23071232 | tf_op jit(solution)/shard_map/pcj,pcbe->jbe/dot_general | solution.py:118
  939.1 53.6 %reduce-scatter.2.cloned.1.call-done = f32[4,128,512]{1,2,0:T(8,128)} async-done(((f32[4,512,512]{1,2,0:T(8,128)}), f32[4,128,512]{1,2,0:T(8,128)}) %reduce-scatter.2.cloned.1.call-update) | async-done | bytes 1048592 | tf_op jit(solution)/shard_map/reduce_scatter | solution.py:143
  998.5 101.8 %all-reduce.2.cloned.1.call-done = f32[4,128,512]{1,2,0:T(8,128)} async-done(((f32[4,128,512]{1,2,0:T(8,128)}), f32[4,128,512]{1,2,0:T(8,128)}) %all-reduce.2.cloned.1.call-update) | async-done | bytes 1048592 | tf_op jit(solution)/shard_map/psum | solution.py:142
  (136 shorter events, 58.4 us)
Async XLA Ops:
  7.2 4.6 copy-start
  7.2 3.8 copy-start.17
  9.2 1.8 copy-start.13
  9.4 1.6 copy-start.11
  10.9 0.8 copy-start.8
  11.0 2.1 copy-start.9
  18.6 12.2 %copy-start.10 = (s32[512,64]{0,1:T(8,128)S(1)}, s32[512,64]{0,1:T(8,128)}, u32[]{:S(2)}) copy-start(s32[512,64]{0,1:T(8,128)} %param.11) | copy-start | bytes 393220
  18.6 108.5 %all-to-all-start = ((bf16[32,2,64,1024]{3,2,1,0:T(8,128)(2,1)}), bf16[32,2,64,1024]{3,2,1,0:T(8,128)(2,1)}, u32[]{:S(2)}, u32[]{:S(2)}) async-start(bf16[32,2,64,1024]{3,2,1,0:T(8,128)(2,1)} %bitcast.152), calls=%async_computation | async-start | bytes 16777216 | tf_op jit(solution)/shard_map/all_to_all | solution.py:89
  30.9 13.6 %copy-start.16 = (s32[64,1]{0,1:T(1,128)S(1)}, s32[64,1]{0,1:T(1,128)}, u32[]{:S(2)}) copy-start(s32[64,1]{0,1:T(1,128)} %concatenate.38) | copy-start | bytes 772
  30.9 14.3 %copy-start.15 = (s32[64]{0:T(128)S(1)}, s32[64]{0:T(128)}, u32[]{:S(2)}) copy-start(s32[64]{0:T(128)} %add.175) | copy-start | bytes 772
  31.0 14.3 %copy-start.18 = (s32[16]{0:T(128)S(1)}, s32[16]{0:T(128)}, u32[]{:S(2)}) copy-start(s32[16]{0:T(128)} %copy-done.17) | copy-start | bytes 196
  211.7 6.9 copy-start.1
  219.8 4.7 copy-start.2
  301.0 5.8 copy-start.3
  306.8 6.2 copy-start.4
  476.2 6.9 copy-start.1
  484.3 4.7 copy-start.2
  565.4 5.8 copy-start.3
  571.3 6.2 copy-start.4
  696.1 212.8 %all-to-all-start.1 = ((f32[32,2,64,1024]{3,1,2,0:T(2,128)}), f32[32,2,64,1024]{3,1,2,0:T(2,128)}, u32[]{:S(2)}, u32[]{:S(2)}) async-start(f32[32,2,64,1024]{3,1,2,0:T(2,128)} %copy.97), calls=%async_computation.1 | async-start | bytes 33554432 | tf_op jit(solution)/shard_map/all_to_all | solution.py:117
  707.4 285.3 %reduce-scatter.2.cloned.1.call-start = ((), (), s32[]{:S(2)}) async-start(), calls=%async_computation.3 | async-start | bytes 5242880 | tf_op jit(solution)/shard_map/reduce_scatter | solution.py:143
  728.7 180.2 %copy-start.12 = (s32[32,16]{0,1:T(8,128)S(1)}, s32[32,16]{0,1:T(8,128)}, u32[]{:S(2)}) copy-start(s32[32,16]{0,1:T(8,128)} %copy-done.11) | copy-start | bytes 6148
  728.7 180.2 %copy-start.14 = (pred[32,16]{0,1:T(8,128)(4,1)S(1)}, pred[32,16]{0,1:T(8,128)(4,1)}, u32[]{:S(2)}) copy-start(pred[32,16]{0,1:T(8,128)(4,1)} %copy-done.13) | copy-start | bytes 1540
  929.8 4.0 copy-start.6
  929.8 4.0 copy-start.7
  931.0 1.4 copy-start.5
  936.3 164.0 %all-reduce.2.cloned.1.call-start = ((), (), s32[]{:S(2)}) async-start(), calls=%async_computation.4 | async-start | bytes 2097152 | tf_op jit(solution)/shard_map/psum | solution.py:142
Sparse Core Ops, SparseCore 0:
  936.4 56.1 reduce-scatter.1
  996.2 104.0 all-reduce.1
where the time goes:
time: 1120 us; the launch traced here: 1110 us
  waiting for transfers between devices  406 us (36%)
  local copies, waits for them, and re-layouts  339 us (30%)
  matrix products  220 us (20%)
  other arithmetic  109 us (10%)
  starting transfers between devices  20.1 us (2%)
  between operations  14.6 us (1%)
    all_to_all x1, waiting for transfers between devices, local(): lax.all_to_all(remote_part, 'verts', split_axis=0, concat_axis=0, tiled=T...  169 us
    psum x1, waiting for transfers between devices, local(): summed_verts = lax.psum(terms, 'verts')  102 us
    all_to_all x1, waiting for transfers between devices, local(): lax.all_to_all(outgoing, 'verts', split_axis=0, concat_axis=0, tiled=True)  81.6 us
    scatter-add x2, other arithmetic, group_step(): return (totals.at[entry_ids].add(both_grads), (attended, grad_q))  74.7 us
    dot_general x2, matrix products, block_pass(): jnp.einsum('ghqk,gqhd->gkhd', dscore, query_blk, preferred_element_type=j...  71 us
    dot_general x2, matrix products, block_pass(): jnp.einsum('ghqk,gkhd->gqhd', dscore, key_blk, preferred_element_type=jnp...  70.5 us
    reshape x2, local copies, waits for them, and re-layouts, group_step(): jnp.stack([grad_keys, grad_values], axis=2)  56.6 us
    another operation x2, local copies, waits for them, and re-layouts, group_step(): jnp.stack([grad_keys, grad_values], axis=2)  55.1 us
  transfers between devices with their start and end apart: 4, of which 4 were waited for; matrix products, arithmetic and copies ran while one was open for 5% of the time, Pallas kernels for 0%

commit v1 on v0

v1 whole, which is shorter than its diff:
```python
import functools
import math

import jax
import jax.numpy as jnp
from jax import lax
from jax.experimental import pallas as pl
from jax.experimental.pallas import tpu as pltpu
from jax.sharding import PartitionSpec as P

H = 8
BS = 64
NNB = 8
CAP = 2

ROWS = 512
HALF = 256

NT = (((1,), (1,)), ((), ()))
TN = (((0,), (0,)), ((), ()))


def dot(a, b):
    return jnp.dot(a, b, preferred_element_type=jnp.float32)


def dot_nt(a, b):
    return lax.dot_general(a, b, NT, preferred_element_type=jnp.float32)


def dot_tn(a, b):
    return lax.dot_general(a, b, TN, preferred_element_type=jnp.float32)


def layer_kernel(
    steps_a,
    steps_b,
    remote,
    scaling,
    entries,
    counts,
    far_ref,
    own_kv_ref,
    wkv_ref,
    q_ref,
    u_ref,
    diag_ref,
    att_ref,
    gq_ref,
    gkv_ref,
    back_ref,
    keys,
    values,
    gkeys,
    gvalues,
):
    step = pl.program_id(0)
    per = ROWS // BS
    own = own_kv_ref.shape[0] // BS
    dim = q_ref.shape[1]

    @pl.when(step == 0)
    def _():
        for b in range(own):
            rows = slice(b * BS, (b + 1) * BS)
            keys[remote + b] = own_kv_ref[rows, :dim]
            values[remote + b] = own_kv_ref[rows, dim:]
            gkeys[remote + b] = jnp.zeros((BS, dim), jnp.float32)
            gvalues[remote + b] = jnp.zeros((BS, dim), jnp.float32)

    @pl.when(step < steps_a)
    def _():
        first = pl.ds(step * per, per)
        both = dot(far_ref[...], wkv_ref[...]).astype(jnp.bfloat16)
        keys[first] = both[:, :dim].reshape(per, BS, dim)
        values[first] = both[:, dim:].reshape(per, BS, dim)
        gkeys[first] = jnp.zeros((per, BS, dim), jnp.float32)
        gvalues[first] = jnp.zeros((per, BS, dim), jnp.float32)

    @pl.when((step >= steps_a) & (step < steps_a + steps_b))
    def _():
        base = (step - steps_a) * NNB
        ids = [entries[base + n] for n in range(NNB)]
        ends = [counts[base + n] for n in range(NNB)]
        place = lax.broadcasted_iota(jnp.int32, (BS, HALF), 0)
        lane_head = lax.broadcasted_iota(jnp.int32, (BS, HALF), 1) // BS
        queries = q_ref[...] * jnp.bfloat16(scaling)
        ups = u_ref[...]
        for half in range(dim // HALF):
            cols = slice(half * HALF, (half + 1) * HALF)
            diag = diag_ref[...]
            qbd = jnp.concatenate([queries[:, cols]] * (HALF // BS), axis=0) * diag
            ubd = jnp.concatenate([ups[:, cols]] * (HALF // BS), axis=0) * diag
            k_all = jnp.concatenate([keys[i, :, cols] for i in ids], axis=0)
            v_all = jnp.concatenate([values[i, :, cols] for i in ids], axis=0)
            scores = dot_nt(k_all, qbd)
            scores = jnp.concatenate(
                [
                    jnp.where(place < ends[n], scores[n * BS : (n + 1) * BS], -1e30)
                    for n in range(NNB)
                ],
                axis=0,
            )
            top = jnp.max(scores, axis=0, keepdims=True)
            raised = jnp.exp(scores - top)
            probs = raised * (1.0 / jnp.sum(raised, axis=0, keepdims=True))
            probs_b = probs.astype(jnp.bfloat16)
            dprob = dot_nt(v_all, ubd)
            inner = jnp.sum(probs * dprob, axis=0, keepdims=True)
            dscore = (probs * (dprob - inner)).astype(jnp.bfloat16)
            att_all = dot_tn(probs_b, v_all)
            gq_all = dot_tn(dscore, k_all)
            att = att_all[:BS]
            gq = gq_all[:BS]
            for h in range(1, HALF // BS):
                rows = slice(h * BS, (h + 1) * BS)
                att = jnp.where(lane_head == h, att_all[rows], att)
                gq = jnp.where(lane_head == h, gq_all[rows], gq)
            att_ref[:, cols] = att.astype(jnp.bfloat16)
            gq_ref[:, cols] = (gq * scaling).astype(jnp.bfloat16)
            grad_v = dot(probs_b, ubd)
            grad_k = dot(dscore, qbd)
            for n in range(NNB):
                rows = slice(n * BS, (n + 1) * BS)
                gkeys[ids[n], :, cols] += grad_k[rows]
                gvalues[ids[n], :, cols] += grad_v[rows]

    @pl.when(step >= steps_a + steps_b)
    def _():
        chunk = step - steps_a - steps_b
        first = pl.ds(chunk * per, per)
        gkv_ref[:, :dim] = gkeys[first].reshape(ROWS, dim).astype(jnp.bfloat16)
        gkv_ref[:, dim:] = gvalues[first].reshape(ROWS, dim).astype(jnp.bfloat16)

        @pl.when(chunk < steps_a)
        def _():
            back_ref[...] = dot_nt(gkv_ref[...], wkv_ref[...]).astype(jnp.bfloat16)


def layer_call(entries, counts, far, own_kv, wkv, queries, ups, scaling):
    far_rows, dim = far.shape
    rows = queries.shape[0]
    blocks = rows // BS
    steps_a = far_rows // ROWS
    steps_c = (far_rows + rows) // ROWS
    steps_b = blocks
    table = (far_rows + rows) // BS
    head = jnp.arange(HALF, dtype=jnp.int32) // BS
    diag = (head[:, None] == head[None, :]).astype(jnp.bfloat16)

    def at_b(i, *_):
        return (jnp.clip(i - steps_a, 0, steps_b - 1), 0)

    def at_c(i, *_):
        return (jnp.maximum(i - steps_a - steps_b, 0), 0)

    def at_back(i, *_):
        return (jnp.clip(i - steps_a - steps_b, 0, steps_a - 1), 0)

    def whole(shape):
        return pl.BlockSpec(shape, lambda i, *_: (0, 0))

    return pl.pallas_call(
        functools.partial(layer_kernel, steps_a, steps_b, far_rows // BS, scaling),
        grid_spec=pltpu.PrefetchScalarGridSpec(
            num_scalar_prefetch=2,
            grid=(steps_a + steps_b + steps_c,),
            in_specs=[
                pl.BlockSpec((ROWS, dim), lambda i, *_: (jnp.minimum(i, steps_a - 1), 0)),
                whole((rows, 2 * dim)),
                whole((dim, 2 * dim)),
                pl.BlockSpec((BS, dim), at_b),
                pl.BlockSpec((BS, dim), at_b),
                whole((HALF, HALF)),
            ],
            out_specs=[
                pl.BlockSpec((BS, dim), at_b),
                pl.BlockSpec((BS, dim), at_b),
                pl.BlockSpec((ROWS, 2 * dim), at_c),
                pl.BlockSpec((ROWS, dim), at_back),
            ],
            scratch_shapes=[
                pltpu.VMEM((table, BS, dim), jnp.bfloat16),
                pltpu.VMEM((table, BS, dim), jnp.bfloat16),
                pltpu.VMEM((table, BS, dim), jnp.float32),
                pltpu.VMEM((table, BS, dim), jnp.float32),
            ],
        ),
        out_shape=[
            jax.ShapeDtypeStruct((rows, dim), jnp.bfloat16),
            jax.ShapeDtypeStruct((rows, dim), jnp.bfloat16),
            jax.ShapeDtypeStruct((far_rows + rows, 2 * dim), jnp.bfloat16),
            jax.ShapeDtypeStruct((far_rows, dim), jnp.bfloat16),
        ],
        compiler_params=pltpu.CompilerParams(vmem_limit_bytes=56 * 2**20),
    )(entries, counts, far, own_kv, wkv, queries, ups, diag)


def combine_kernel(per, send_ref, base_ref, ret_ref, out_ref, acc):
    step = pl.program_id(0)

    @pl.when(step == 0)
    def _():
        acc[...] = base_ref[...]

    for i in range(per):
        acc[send_ref[step * per + i]] += ret_ref[i].astype(jnp.float32)

    @pl.when(step == pl.num_programs(0) - 1)
    def _():
        out_ref[...] = acc[...].astype(jnp.bfloat16)


def combine_call(send, base, returned):
    blocks, _, dim = base.shape
    total = returned.shape[0]
    per = 8
    return pl.pallas_call(
        functools.partial(combine_kernel, per),
        grid_spec=pltpu.PrefetchScalarGridSpec(
            num_scalar_prefetch=1,
            grid=(total // per,),
            in_specs=[
                pl.BlockSpec((blocks, BS, dim), lambda i, *_: (0, 0, 0)),
                pl.BlockSpec((per, BS, dim), lambda i, *_: (i, 0, 0)),
            ],
            out_specs=pl.BlockSpec((blocks, BS, dim), lambda i, *_: (0, 0, 0)),
            scratch_shapes=[pltpu.VMEM((blocks, BS, dim), jnp.float32)],
        ),
        out_shape=jax.ShapeDtypeStruct((blocks, BS, dim), jnp.bfloat16),
        compiler_params=pltpu.CompilerParams(vmem_limit_bytes=32 * 2**20),
    )(send, base, returned)


def local(feats, weights, grad_out, neighbours, valid):
    nparts = lax.axis_size("verts")
    me = lax.axis_index("verts")
    _, rows, dim = feats.shape
    blocks = rows // BS
    scaling = 1.0 / math.sqrt(dim // H)
    part_ids = jnp.arange(nparts, dtype=jnp.int32)
    inputs_now = feats[0]
    cotangent = grad_out[0]
    w_kv = jnp.concatenate([weights[1], weights[2]], axis=1)

    theirs = neighbours.reshape(nparts, blocks * NNB)
    mine = (theirs // blocks == me) & (part_ids[:, None] != me)
    place = theirs % blocks
    low = jnp.min(jnp.where(mine, place, blocks), axis=1)
    high = jnp.max(jnp.where(mine, place, -1), axis=1)
    send = jnp.stack([low % blocks, jnp.maximum(high, 0)], axis=1).reshape(-1)

    lists = lax.dynamic_slice_in_dim(neighbours, me * blocks, blocks, 0).reshape(-1)
    owner = lists // blocks
    named = owner[:, None] == part_ids[None, :]
    lower = jnp.min(jnp.where(named, (lists % blocks)[:, None], blocks), axis=0)
    slot = (jnp.sum(jnp.where(named, lower[None, :], 0), axis=1) != lists % blocks).astype(jnp.int32)
    entries = jnp.where(owner == me, nparts * CAP + lists % blocks, owner * CAP + slot)
    counts = jnp.sum(valid, axis=1)[lists]

    far = lax.all_to_all(
        inputs_now.reshape(blocks, BS, dim)[send].reshape(nparts, CAP, BS, dim),
        "verts",
        split_axis=0,
        concat_axis=0,
        tiled=True,
    ).reshape(nparts * CAP * BS, dim)

    queries = dot(inputs_now, weights[0]).astype(jnp.bfloat16)
    ups = dot_nt(cotangent, weights[3]).astype(jnp.bfloat16)
    own_kv = dot(inputs_now, w_kv).astype(jnp.bfloat16)

    attended, grad_q, grad_kv, back = layer_call(
        entries, counts, far, own_kv, w_kv, queries, ups, scaling
    )
    returned = lax.all_to_all(
        back.reshape(nparts, CAP, BS, dim), "verts", split_axis=0, concat_axis=0, tiled=True
    ).reshape(nparts * CAP, BS, dim)

    attn_out = dot(attended, weights[3]).astype(jnp.bfloat16)
    own_grad = grad_kv[nparts * CAP * BS :]
    base = dot_nt(grad_q, weights[0]) + dot_nt(own_grad, w_kv)
    grad_wkv = dot_tn(inputs_now, own_grad) + dot_tn(far, grad_kv[: nparts * CAP * BS])
    terms = jnp.stack(
        [
            dot_tn(inputs_now, grad_q),
            grad_wkv[:, :dim],
            grad_wkv[:, dim:],
            dot_tn(attended, cotangent),
        ]
    )
    shared = lax.psum_scatter(terms, "dp", scatter_dimension=1, tiled=True)
    flat = shared.reshape(-1, dim)
    pieces = lax.psum_scatter(flat, "verts", scatter_dimension=0, tiled=True)
    grad_weights = lax.all_gather(pieces, "verts", axis=0, tiled=True).reshape(shared.shape)

    grad_feats = combine_call(send, base.reshape(blocks, BS, dim), returned)
    return (attn_out[None], grad_feats.reshape(1, rows, dim), grad_weights)


def solution(mesh):
    in_specs = (P("dp", "verts", None), P(), P("dp", "verts", None), P(), P())
    out_specs = (P("dp", "verts", None), P("dp", "verts", None), P(None, "dp", None))
    return jax.shard_map(local, mesh=mesh, in_specs=in_specs, out_specs=out_specs, check_vma=False)
```

time: 1120 us -> 322 us (0.29)
  local copies, waits for them, and re-layouts: 339 us -> 13.3 us
  waiting for transfers between devices: 406 us -> 186 us
  matrix products: 220 us -> 26.9 us
  other arithmetic: 109 us -> 6.25 us
  Pallas kernels: 0 us -> 57.6 us
    all_to_all x2, waiting for transfers between devices: 251 us -> 37.3 us  [the longest x1 37.3 us: local(): lax.all_to_all(inputs_now.reshape(blocks, BS, dim)[send].reshape(nparts,...]
    dot_general x22 -> x10, matrix products: 220 us -> 26.9 us  [the longest x4 13.5 us: dot_tn(): return lax.dot_general(a, b, TN, preferred_element_type=jnp.float32)]
    reshape x12 -> x4, local copies, waits for them, and re-layouts: 130 us -> 0.38 us  [the longest x2 0.2 us: local(): send = jnp.stack([low % blocks, jnp.maximum(high, 0)], axis=1).reshape(-1)]
    psum x1 -> x0, waiting for transfers between devices: 102 us -> none  [local(): summed_verts = lax.psum(terms, 'verts')]
    scatter-add x2 -> x0, other arithmetic: 74.7 us -> none  [group_step(): return (totals.at[entry_ids].add(both_grads), (attended, grad_q))]
    reduce_scatter x1 -> x2, waiting for transfers between devices: 53.6 us -> 117 us  [the longest x1 77.1 us: local(): pieces = lax.psum_scatter(flat, 'verts', scatter_dimension=0, tiled=True)]
    while x21 -> x0, local copies, waits for them, and re-layouts: 63.1 us -> none
    pallas_call x0 -> x2, Pallas kernels: none -> 57.6 us  [the longest x1 51 us: layer_call(): pl.pallas_call(functools.partial(layer_kernel, steps_a, steps_b, far_rows...]
  transfers between devices with their start and end apart: 4 -> 5, of which waited for: 4 -> 4; matrix products, arithmetic and copies ran while one was open for 5% -> 7% of each run, Pallas kernels for 0% -> 2%
where the time goes in v1:
time: 322 us
  waiting for transfers between devices  186 us (58%)
  Pallas kernels  57.6 us (18%)
  matrix products  26.9 us (8%)
  starting transfers between devices  17 us (5%)
  between operations  14 us (4%)
  local copies, waits for them, and re-layouts  13.3 us (4%)
  other arithmetic  6.25 us (2%)
    reduce_scatter x1, waiting for transfers between devices, local(): pieces = lax.psum_scatter(flat, 'verts', scatter_dimension=0, tiled=True)  77.1 us
    pallas_call x1, Pallas kernels, layer_call(): pl.pallas_call(functools.partial(layer_kernel, steps_a, steps_b, far_rows...  51 us
    reduce_scatter x1, waiting for transfers between devices, local(): shared = lax.psum_scatter(terms, 'dp', scatter_dimension=1, tiled=True)  39.7 us
    all_to_all x1, waiting for transfers between devices, local(): lax.all_to_all(inputs_now.reshape(blocks, BS, dim)[send].reshape(nparts,...  37.3 us
    all_gather x1, waiting for transfers between devices, local(): lax.all_gather(pieces, 'verts', axis=0, tiled=True).reshape(shared.shape)  32.2 us
    dot_general x4, matrix products, dot_tn(): return lax.dot_general(a, b, TN, preferred_element_type=jnp.float32)  13.5 us
    all_to_all x1, starting transfers between devices, local(): lax.all_to_all(inputs_now.reshape(blocks, BS, dim)[send].reshape(nparts,...  8.78 us
    all_to_all x1, starting transfers between devices, local(): lax.all_to_all(back.reshape(nparts, CAP, BS, dim), 'verts', split_axis=0,...  7.96 us
  transfers between devices with their start and end apart: 5, of which 4 were waited for; matrix products, arithmetic and copies ran while one was open for 7% of the time, Pallas kernels for 2%

profile of v1, /device:TPU:1, one launch (start us, length us, event | category | flops | bytes accessed | tf_op | source)
XLA Modules:
  0.0 321.5 jit_solution(1343789724282784025)
XLA Ops:
  7.2 0.1 and.101
  7.3 0.1 and.102
  7.4 0.9 select_reduce_fusion.1
  8.2 0.1 reduce_min.29
  8.3 0.1 reduce_min.30
  8.4 0.1 reduce_max.14
  8.5 0.1 reduce_max.18
  8.7 0.1 copy.25
  8.8 0.1 reshape.228
  8.9 2.7 gather_fusion.1
  11.6 8.8 %all-to-all-start = ((bf16[32,2,64,512]{3,2,1,0:T(8,128)(2,1)}), bf16[32,2,64,512]{3,2,1,0:T(8,128)(2,1)}, u32[]{:S(2)}, u32[]{:S(2)}) async-start(bf16[32,2,64,512]{3,2,1,0:T(8,128)(2,1)} %bitcast.68), calls=%async_computation | async-start | bytes 8388608 | tf_op jit(solution)/shard_map/all_to_all | solution.py:261
  20.4 0.0 reduce-scatter.3.cloned.1.call-start
  20.5 0.8 constant_dynamic-slice_fusion
  21.2 0.1 copy.23
  21.3 0.1 reshape.227
  21.4 0.1 reshape.226
  21.6 1.8 gather_fusion
  23.4 0.1 select_reduce_fusion.3
  23.5 0.1 select_reduce_fusion.2
  23.6 1.4 slice_bitcast_fusion.3
  25.1 1.1 pad_maximum_fusion.1.wkv_ref
  26.1 0.5 compare_select_fusion.4.entries
  26.7 0.7 compare_convert_fusion.diag_ref
  27.4 1.7 convolution_convert_fusion.2.q_ref
  29.1 1.7 convolution_convert_fusion.1.u_ref
  30.8 2.6 convert_bitcast_fusion.own_kv_ref
  33.4 37.3 %all-to-all-done = bf16[32,2,64,512]{3,2,1,0:T(8,128)(2,1)} async-done(((bf16[32,2,64,512]{3,2,1,0:T(8,128)(2,1)}), bf16[32,2,64,512]{3,2,1,0:T(8,128)(2,1)}, u32[]{:S(2)}, u32[]{:S(2)}) %all-to-all-start) | async-done | bytes 4194336 | tf_op jit(solution)/shard_map/all_to_all | solution.py:261
  70.7 51.0 %shard_map.76 = (bf16[1024,512]{1,0:T(8,128)(2,1)}, bf16[1024,512]{1,0:T(8,128)(2,1)}, bf16[5120,1024]{1,0:T(8,128)(2,1)}, bf16[4096,512]{1,0:T(8,128)(2,1)}) custom-call(s32[128]{0:T(128)} %compare_select_fusion.4.entries, s32[128]{0:T(128)} %gather_fusion, bf16[4096,512]{1,0:T(8,128)(2,1)} %bitcast.6.far_ref, ...), custom_call_target="tpu_custom_call" | custom-call | tf_op jit(solution)/shard_map/pallas_call | solution.py:163
  121.7 2.1 convolution_bitcast_fusion
  123.8 0.7 convolution_bitcast_fusion.1
  124.5 3.2 fusion.2
  127.7 0.7 copy-done.5
  128.4 7.5 %bitcast_add_fusion = f32[512,1024]{0,1:T(8,128)S(1)} fusion(f32[1024,512]{1,0:T(8,128)S(1)} %fusion.2, bf16[4096,512]{1,0:T(8,128)(2,1)} %bitcast.6.far_ref, bf16[5120,1024]{1,0:T(8,128)(2,1)S(1)} %copy-done.5), kind=kOutput, calls=%fused_computation.5 | convolution fusion | flops 4295491584 | bytes 16777216 | tf_op jit(solution)/shard_map/dot_general | solution.py:32
  135.9 0.2 slice_bitcast_fusion.1
  136.1 2.5 pad_maximum_fusion
  138.6 8.0 %all-to-all-start.1 = ((bf16[32,2,64,512]{3,2,1,0:T(8,128)(2,1)}), bf16[32,2,64,512]{3,2,1,0:T(8,128)(2,1)}, u32[]{:S(2)}, u32[]{:S(2)}) async-start(bf16[32,2,64,512]{3,2,1,0:T(8,128)(2,1)} %bitcast.69), calls=%async_computation.1 | async-start | bytes 8388608 | tf_op jit(solution)/shard_map/all_to_all | solution.py:276
  146.6 0.2 reduce-scatter.5.cloned.1.call-start
  146.9 39.7 %reduce-scatter.3.cloned.1.call-done = f32[4,128,512]{1,2,0:T(8,128)} async-done(((f32[4,512,512]{1,2,0:T(8,128)}), f32[4,128,512]{1,2,0:T(8,128)}) %reduce-scatter.3.cloned.1.call-update) | async-done | bytes 1048592 | tf_op jit(solution)/shard_map/reduce_scatter | solution.py:292
  186.6 2.5 copy.30
  189.1 0.0 all-gather.2.cloned.1.call-start
  189.2 77.1 %reduce-scatter.5.cloned.1.call-done = f32[16,512]{1,0:T(8,128)} async-done(((f32[512,512]{1,0:T(8,128)}), f32[16,512]{1,0:T(8,128)}) %reduce-scatter.5.cloned.1.call-update) | async-done | bytes 32784 | tf_op jit(solution)/shard_map/reduce_scatter | solution.py:294
  266.3 0.1 reshape.231.send_ref
  266.4 2.7 fusion.8
  269.2 3.0 fusion.4
  272.1 1.8 convolution_add_fusion
  273.9 6.6 %shard_map.77 = bf16[16,64,512]{2,1,0:T(8,128)(2,1)} custom-call(s32[64]{0:T(128)S(1)} %reshape.231.send_ref, f32[16,64,512]{2,1,0:T(8,128)S(1)} %bitcast.67, bf16[64,64,512]{2,1,0:T(8,128)(2,1)} %bitcast.17.ret_ref), custom_call_target="tpu_custom_call" | custom-call | tf_op jit(solution)/shard_map/pallas_call | solution.py:218
  280.6 32.2 %all-gather.2.cloned.1.call-done = f32[512,512]{1,0:T(8,128)} async-done(((f32[16,512]{1,0:T(8,128)}), f32[512,512]{1,0:T(8,128)}) %all-gather.2.cloned.1.call-update) | async-done | bytes 1048592 | tf_op jit(solution)/shard_map/all_gather | solution.py:295
  312.7 2.3 copy.35
  (30 shorter events, 0.2 us)
Async XLA Ops:
  7.2 1.7 copy-start
  11.6 9.9 %copy-start.4 = (s32[512,64]{0,1:T(8,128)S(1)}, s32[512,64]{0,1:T(8,128)}, u32[]{:S(2)}) copy-start(s32[512,64]{0,1:T(8,128)} %param.9) | copy-start | bytes 393220
  11.6 59.0 %all-to-all-start = ((bf16[32,2,64,512]{3,2,1,0:T(8,128)(2,1)}), bf16[32,2,64,512]{3,2,1,0:T(8,128)(2,1)}, u32[]{:S(2)}, u32[]{:S(2)}) async-start(bf16[32,2,64,512]{3,2,1,0:T(8,128)(2,1)} %bitcast.68), calls=%async_computation | async-start | bytes 8388608 | tf_op jit(solution)/shard_map/all_to_all | solution.py:261
  20.4 166.1 %reduce-scatter.3.cloned.1.call-start = ((), (), s32[]{:S(2)}) async-start(), calls=%async_computation.4 | async-start | bytes 5242880 | tf_op jit(solution)/shard_map/reduce_scatter | solution.py:292
  23.6 3.8 %copy-start.1 = (bf16[4,512,512]{2,1,0:T(8,128)(2,1)S(1)}, bf16[4,512,512]{2,1,0:T(8,128)(2,1)}, u32[]{:S(2)}) copy-start(bf16[4,512,512]{2,1,0:T(8,128)(2,1)} %param.6) | copy-start | bytes 6291460
  25.0 4.1 %copy-start.6 = (bf16[1,1024,512]{2,1,0:T(8,128)(2,1)S(1)}, bf16[1,1024,512]{2,1,0:T(8,128)(2,1)}, u32[]{:S(2)}) copy-start(bf16[1,1024,512]{2,1,0:T(8,128)(2,1)} %param.7) | copy-start | bytes 3145732
  121.7 2.1 copy-start.2
  123.8 4.6 %copy-start.5 = (bf16[5120,1024]{1,0:T(8,128)(2,1)S(1)}, bf16[5120,1024]{1,0:T(8,128)(2,1)}, u32[]{:S(2)}) copy-start(bf16[5120,1024]{1,0:T(8,128)(2,1)} %get-tuple-element.9) | copy-start | bytes 31457284
  138.6 135.3 %all-to-all-start.1 = ((bf16[32,2,64,512]{3,2,1,0:T(8,128)(2,1)}), bf16[32,2,64,512]{3,2,1,0:T(8,128)(2,1)}, u32[]{:S(2)}, u32[]{:S(2)}) async-start(bf16[32,2,64,512]{3,2,1,0:T(8,128)(2,1)} %bitcast.69), calls=%async_computation.1 | async-start | bytes 8388608 | tf_op jit(solution)/shard_map/all_to_all | solution.py:276
  146.6 119.8 %copy-start.7 = (bf16[1024,512]{1,0:T(8,128)(2,1)S(1)}, bf16[1024,512]{1,0:T(8,128)(2,1)}, u32[]{:S(2)}) copy-start(bf16[1024,512]{1,0:T(8,128)(2,1)} %get-tuple-element.7) | copy-start | bytes 3145732
  146.6 119.7 %reduce-scatter.5.cloned.1.call-start = ((), (), s32[]{:S(2)}) async-start(), calls=%async_computation.5 | async-start | bytes 1081344 | tf_op jit(solution)/shard_map/reduce_scatter | solution.py:294
  189.1 123.6 %all-gather.2.cloned.1.call-start = ((), (), s32[]{:S(2)}) async-start(), calls=%async_computation.6 | async-start | bytes 1081344 | tf_op jit(solution)/shard_map/all_gather | solution.py:295
  269.2 3.0 copy-start.3
Sparse Core Ops, SparseCore 0:
  138.8 47.7 reduce-scatter.2
  191.0 75.2 reduce-scatter.4
  268.6 44.0 all-gather.1

commit v2 on v1

--- a/solution.py
+++ b/solution.py
@@ -40,6 +40,8 @@
     entries,
     counts,
     far_ref,
+    own_ref,
+    cot_ref,
     own_kv_ref,
     wkv_ref,
     q_ref,
@@ -47,12 +49,16 @@
     diag_ref,
     att_ref,
     gq_ref,
-    gkv_ref,
+    own_grad_ref,
     back_ref,
+    qo_ref,
+    kv_ref,
     keys,
     values,
     gkeys,
     gvalues,
+    att_all,
+    gq_all,
 ):
     step = pl.program_id(0)
     per = ROWS // BS
@@ -79,7 +85,8 @@
 
     @pl.when((step >= steps_a) & (step < steps_a + steps_b))
     def _():
-        base = (step - steps_a) * NNB
+        block = step - steps_a
+        base = block * NNB
         ids = [entries[base + n] for n in range(NNB)]
         ends = [counts[base + n] for n in range(NNB)]
         place = lax.broadcasted_iota(jnp.int32, (BS, HALF), 0)
@@ -108,16 +115,20 @@
             dprob = dot_nt(v_all, ubd)
             inner = jnp.sum(probs * dprob, axis=0, keepdims=True)
             dscore = (probs * (dprob - inner)).astype(jnp.bfloat16)
-            att_all = dot_tn(probs_b, v_all)
-            gq_all = dot_tn(dscore, k_all)
-            att = att_all[:BS]
-            gq = gq_all[:BS]
+            att_wide = dot_tn(probs_b, v_all)
+            gq_wide = dot_tn(dscore, k_all)
+            att = att_wide[:BS]
+            gq = gq_wide[:BS]
             for h in range(1, HALF // BS):
                 rows = slice(h * BS, (h + 1) * BS)
-                att = jnp.where(lane_head == h, att_all[rows], att)
-                gq = jnp.where(lane_head == h, gq_all[rows], gq)
-            att_ref[:, cols] = att.astype(jnp.bfloat16)
-            gq_ref[:, cols] = (gq * scaling).astype(jnp.bfloat16)
+                att = jnp.where(lane_head == h, att_wide[rows], att)
+                gq = jnp.where(lane_head == h, gq_wide[rows], gq)
+            att = att.astype(jnp.bfloat16)
+            gq = (gq * scaling).astype(jnp.bfloat16)
+            att_ref[:, cols] = att
+            gq_ref[:, cols] = gq
+            att_all[block, :, cols] = att
+            gq_all[block, :, cols] = gq
             grad_v = dot(probs_b, ubd)
             grad_k = dot(dscore, qbd)
             for n in range(NNB):
@@ -129,15 +140,34 @@
     def _():
         chunk = step - steps_a - steps_b
         first = pl.ds(chunk * per, per)
-        gkv_ref[:, :dim] = gkeys[first].reshape(ROWS, dim).astype(jnp.bfloat16)
-        gkv_ref[:, dim:] = gvalues[first].reshape(ROWS, dim).astype(jnp.bfloat16)
+        grad_k = gkeys[first].reshape(ROWS, dim).astype(jnp.bfloat16)
+        grad_v = gvalues[first].reshape(ROWS, dim).astype(jnp.bfloat16)
+
+        @pl.when(chunk == 0)
+        def _():
+            kv_ref[...] = jnp.zeros_like(kv_ref)
+            qo_ref[...] = jnp.zeros_like(qo_ref)
 
         @pl.when(chunk < steps_a)
         def _():
-            back_ref[...] = dot_nt(gkv_ref[...], wkv_ref[...]).astype(jnp.bfloat16)
-
-
-def layer_call(entries, counts, far, own_kv, wkv, queries, ups, scaling):
+            back_ref[...] = (
+                dot_nt(grad_k, wkv_ref[:, :dim]) + dot_nt(grad_v, wkv_ref[:, dim:])
+            ).astype(jnp.bfloat16)
+            kv_ref[0] += dot_tn(far_ref[...], grad_k)
+            kv_ref[1] += dot_tn(far_ref[...], grad_v)
+
+        @pl.when(chunk >= steps_a)
+        def _():
+            own_grad_ref[:, :dim] = grad_k
+            own_grad_ref[:, dim:] = grad_v
+            here = pl.ds((chunk - steps_a) * per, per)
+            kv_ref[0] += dot_tn(own_ref[...], grad_k)
+            kv_ref[1] += dot_tn(own_ref[...], grad_v)
+            qo_ref[0] += dot_tn(own_ref[...], gq_all[here].reshape(ROWS, dim))
+            qo_ref[1] += dot_tn(att_all[here].reshape(ROWS, dim), cot_ref[...])
+
+
+def layer_call(entries, counts, far, own, cot, own_kv, wkv, queries, ups, scaling):
     far_rows, dim = far.shape
     rows = queries.shape[0]
     blocks = rows // BS
@@ -148,17 +178,20 @@
     head = jnp.arange(HALF, dtype=jnp.int32) // BS
     diag = (head[:, None] == head[None, :]).astype(jnp.bfloat16)
 
+    def at_far(i, *_):
+        return (jnp.where(i < steps_a + steps_b, jnp.minimum(i, steps_a - 1), jnp.minimum(i - steps_a - steps_b, steps_a - 1)), 0)
+
     def at_b(i, *_):
         return (jnp.clip(i - steps_a, 0, steps_b - 1), 0)
 
-    def at_c(i, *_):
-        return (jnp.maximum(i - steps_a - steps_b, 0), 0)
+    def at_own(i, *_):
+        return (jnp.maximum(i - 2 * steps_a - steps_b, 0), 0)
 
     def at_back(i, *_):
         return (jnp.clip(i - steps_a - steps_b, 0, steps_a - 1), 0)
 
     def whole(shape):
-        return pl.BlockSpec(shape, lambda i, *_: (0, 0))
+        return pl.BlockSpec(shape, lambda i, *_: (0,) * len(shape), pipeline_mode=pl.Buffered(1))
 
     return pl.pallas_call(
         functools.partial(layer_kernel, steps_a, steps_b, far_rows // BS, scaling),
@@ -166,7 +199,9 @@
             num_scalar_prefetch=2,
             grid=(steps_a + steps_b + steps_c,),
             in_specs=[
-                pl.BlockSpec((ROWS, dim), lambda i, *_: (jnp.minimum(i, steps_a - 1), 0)),
+                pl.BlockSpec((ROWS, dim), at_far),
+                pl.BlockSpec((ROWS, dim), at_own),
+                pl.BlockSpec((ROWS, dim), at_own),
                 whole((rows, 2 * dim)),
                 whole((dim, 2 * dim)),
                 pl.BlockSpec((BS, dim), at_b),
@@ -176,24 +211,30 @@
             out_specs=[
                 pl.BlockSpec((BS, dim), at_b),
                 pl.BlockSpec((BS, dim), at_b),
-                pl.BlockSpec((ROWS, 2 * dim), at_c),
+                pl.BlockSpec((ROWS, 2 * dim), at_own),
                 pl.BlockSpec((ROWS, dim), at_back),
+                pl.BlockSpec((2, dim, dim), lambda i, *_: (0, 0, 0)),
+                pl.BlockSpec((2, dim, dim), lambda i, *_: (0, 0, 0)),
             ],
             scratch_shapes=[
                 pltpu.VMEM((table, BS, dim), jnp.bfloat16),
                 pltpu.VMEM((table, BS, dim), jnp.bfloat16),
                 pltpu.VMEM((table, BS, dim), jnp.float32),
                 pltpu.VMEM((table, BS, dim), jnp.float32),
+                pltpu.VMEM((blocks, BS, dim), jnp.bfloat16),
+                pltpu.VMEM((blocks, BS, dim), jnp.bfloat16),
             ],
         ),
         out_shape=[
             jax.ShapeDtypeStruct((rows, dim), jnp.bfloat16),
             jax.ShapeDtypeStruct((rows, dim), jnp.bfloat16),
-            jax.ShapeDtypeStruct((far_rows + rows, 2 * dim), jnp.bfloat16),
+            jax.ShapeDtypeStruct((rows, 2 * dim), jnp.bfloat16),
             jax.ShapeDtypeStruct((far_rows, dim), jnp.bfloat16),
+            jax.ShapeDtypeStruct((2, dim, dim), jnp.float32),
+            jax.ShapeDtypeStruct((2, dim, dim), jnp.float32),
         ],
-        compiler_params=pltpu.CompilerParams(vmem_limit_bytes=56 * 2**20),
-    )(entries, counts, far, own_kv, wkv, queries, ups, diag)
+        compiler_params=pltpu.CompilerParams(vmem_limit_bytes=58 * 2**20),
+    )(entries, counts, far, own, cot, own_kv, wkv, queries, ups, diag)
 
 
 def combine_kernel(per, send_ref, base_ref, ret_ref, out_ref, acc):
@@ -232,6 +273,42 @@
     )(send, base, returned)
 
 
+def sum_weights(qo_terms, kv_terms, nparts, me, returned):
+    first = me % 2 == 0
+    up = [(v, v + 1) for v in range(0, nparts, 2)]
+    down = [(v + 1, v) for v in range(0, nparts, 2)]
+    qo_other = lax.ppermute(qo_terms, "verts", down)
+    kv_other = lax.ppermute(kv_terms, "verts", up)
+    half = jnp.where(first, qo_terms + qo_other, kv_terms + kv_other)
+    half = lax.psum_scatter(half, "dp", scatter_dimension=1, tiled=True)
+    half, returned = lax.optimization_barrier((half, returned))
+    pair, rows, dim = half.shape
+    chips = nparts // 2
+    groups = [list(range(c, nparts, 2)) for c in range(2)]
+    piece = pair * rows // chips
+    parts = lax.all_to_all(
+        half.reshape(chips, piece, dim).astype(jnp.bfloat16),
+        "verts",
+        split_axis=0,
+        concat_axis=0,
+        axis_index_groups=groups,
+        tiled=True,
+    )
+    total = jnp.sum(parts.astype(jnp.float32), axis=0).astype(jnp.bfloat16)
+    whole = lax.all_to_all(
+        jnp.broadcast_to(total[None], (chips, piece, dim)),
+        "verts",
+        split_axis=0,
+        concat_axis=0,
+        axis_index_groups=groups,
+        tiled=True,
+    ).reshape(pair, rows, dim)
+    other = lax.ppermute(whole, "verts", up + down)
+    q_o = jnp.where(first, whole, other).astype(jnp.float32)
+    k_v = jnp.where(first, other, whole).astype(jnp.float32)
+    return jnp.concatenate([q_o[:1], k_v, q_o[1:]], axis=0), returned
+
+
 def local(feats, weights, grad_out, neighbours, valid):
     nparts = lax.axis_size("verts")
     me = lax.axis_index("verts")
@@ -270,29 +347,16 @@
     ups = dot_nt(cotangent, weights[3]).astype(jnp.bfloat16)
     own_kv = dot(inputs_now, w_kv).astype(jnp.bfloat16)
 
-    attended, grad_q, grad_kv, back = layer_call(
-        entries, counts, far, own_kv, w_kv, queries, ups, scaling
+    attended, grad_q, own_grad, back, qo_terms, kv_terms = layer_call(
+        entries, counts, far, inputs_now, cotangent, own_kv, w_kv, queries, ups, scaling
     )
     returned = lax.all_to_all(
         back.reshape(nparts, CAP, BS, dim), "verts", split_axis=0, concat_axis=0, tiled=True
     ).reshape(nparts * CAP, BS, dim)
 
     attn_out = dot(attended, weights[3]).astype(jnp.bfloat16)
-    own_grad = grad_kv[nparts * CAP * BS :]
     base = dot_nt(grad_q, weights[0]) + dot_nt(own_grad, w_kv)
-    grad_wkv = dot_tn(inputs_now, own_grad) + dot_tn(far, grad_kv[: nparts * CAP * BS])
-    terms = jnp.stack(
-        [
-            dot_tn(inputs_now, grad_q),
-            grad_wkv[:, :dim],
-            grad_wkv[:, dim:],
-            dot_tn(attended, cotangent),
-        ]
-    )
-    shared = lax.psum_scatter(terms, "dp", scatter_dimension=1, tiled=True)
-    flat = shared.reshape(-1, dim)
-    pieces = lax.psum_scatter(flat, "verts", scatter_dimension=0, tiled=True)
-    grad_weights = lax.all_gather(pieces, "verts", axis=0, tiled=True).reshape(shared.shape)
+    grad_weights, returned = sum_weights(qo_terms, kv_terms, nparts, me, returned)
 
     grad_feats = combine_call(send, base.reshape(blocks, BS, dim), returned)
     return (attn_out[None], grad_feats.reshape(1, rows, dim), grad_weights)

time: 322 us -> 249 us (0.77)
  waiting for transfers between devices: 186 us -> 55.6 us
  blocking collectives: 0 us -> 55.6 us
  matrix products: 26.9 us -> 13.8 us
  starting transfers between devices: 17 us -> 26.2 us
  other arithmetic: 6.25 us -> 11.9 us
  local copies, waits for them, and re-layouts: 13.3 us -> 8.25 us
  Pallas kernels: 57.6 us -> 62.6 us
    reduce_scatter x2 -> x1, waiting for transfers between devices: 117 us -> 0.01 us  [sum_weights(): half = lax.psum_scatter(half, 'dp', scatter_dimension=1, tiled=True)]
    all_to_all x0 -> x1, blocking collectives: none -> 55.6 us  [local(): lax.all_to_all(back.reshape(nparts, CAP, BS, dim), 'verts', split_axis=0,...]
    all_gather x1 -> x0, waiting for transfers between devices: 32.2 us -> none  [local(): lax.all_gather(pieces, 'verts', axis=0, tiled=True).reshape(shared.shape)]
    dot_general x4 -> x0, matrix products: 13.5 us -> none  [dot_tn(): return lax.dot_general(a, b, TN, preferred_element_type=jnp.float32)]
    all_to_all x1 -> x2, waiting for transfers between devices: 0.01 us -> 11.9 us  [the longest x1 7.44 us: sum_weights(): lax.all_to_all(half.reshape(chips, piece, dim).astype(jnp.bfloat16), 'ver...]
    ppermute x0 -> x3, starting transfers between devices: none -> 10.1 us  [the longest x1 5.57 us: sum_weights(): qo_other = lax.ppermute(qo_terms, 'verts', down)]
    pallas_call x1, Pallas kernels: 51 us -> 59.9 us  [layer_call(): pl.pallas_call(functools.partial(layer_kernel, steps_a, steps_b, far_rows...]
    select_n x0 -> x1, other arithmetic: none -> 5.22 us  [sum_weights(): half = jnp.where(first, qo_terms + qo_other, kv_terms + kv_other)]
  transfers between devices with their start and end apart: 5 -> 7, of which waited for: 4 -> 5; matrix products, arithmetic and copies ran while one was open for 7% -> 8% of each run, Pallas kernels for 2% -> 1%
where the time goes in v2:
time: 249 us; the launch traced here: 248 us
  Pallas kernels  62.6 us (25%)
  waiting for transfers between devices  55.6 us (22%)
  blocking collectives  55.6 us (22%)
  starting transfers between devices  26.2 us (11%)
  between operations  14.3 us (6%)
  matrix products  13.8 us (6%)
  other arithmetic  11.9 us (5%)
  local copies, waits for them, and re-layouts  8.25 us (3%)
    pallas_call x1, Pallas kernels, layer_call(): pl.pallas_call(functools.partial(layer_kernel, steps_a, steps_b, far_rows...  59.9 us
    all_to_all x1, blocking collectives, local(): lax.all_to_all(back.reshape(nparts, CAP, BS, dim), 'verts', split_axis=0,...  55.6 us
    all_to_all x1, waiting for transfers between devices, local(): lax.all_to_all(inputs_now.reshape(blocks, BS, dim)[send].reshape(nparts,...  38.6 us
    all_to_all x1, starting transfers between devices, local(): lax.all_to_all(inputs_now.reshape(blocks, BS, dim)[send].reshape(nparts,...  8.78 us
    all_to_all x1, waiting for transfers between devices, sum_weights(): lax.all_to_all(half.reshape(chips, piece, dim).astype(jnp.bfloat16), 'ver...  7.44 us
    dot_general x3, matrix products, dot(): return jnp.dot(a, b, preferred_element_type=jnp.float32)  6.97 us
    dot_general x3, matrix products, dot_nt(): return lax.dot_general(a, b, NT, preferred_element_type=jnp.float32)  6.87 us
    ppermute x1, starting transfers between devices, sum_weights(): qo_other = lax.ppermute(qo_terms, 'verts', down)  5.57 us
  transfers between devices with their start and end apart: 7, of which 5 were waited for; matrix products, arithmetic and copies ran while one was open for 8% of the time, Pallas kernels for 1%

profile of v2, /device:TPU:1, one launch (start us, length us, event | category | flops | bytes accessed | tf_op | source)
XLA Modules:
  0.0 248.2 jit_solution(12824496515450383434)
XLA Ops:
  7.2 0.1 and.106
  7.3 0.1 and.107
  7.4 0.8 select_reduce_fusion.1
  8.1 0.1 reduce_min.29
  8.2 0.1 reduce_min.30
  8.3 0.1 reduce_max.14
  8.4 0.1 reduce_max.18
  8.6 0.1 copy.20
  8.7 0.1 reshape.228
  8.8 4.0 %gather_fusion.1 = bf16[64,64,512]{2,1,0:T(8,128)(2,1)} fusion(bf16[16,64,512]{2,1,0:T(8,128)(2,1)} %bitcast.51, s32[1024]{0:T(1024)S(1)} %pad_clamp_fusion), kind=kCustom, calls=%fused_computation.1 | custom fusion | bytes 8388864 | tf_op jit(solution)/shard_map/gather | solution.py:339
  12.8 8.8 %all-to-all-start = ((bf16[32,2,64,512]{3,2,1,0:T(8,128)(2,1)}), bf16[32,2,64,512]{3,2,1,0:T(8,128)(2,1)}, u32[]{:S(2)}, u32[]{:S(2)}) async-start(bf16[32,2,64,512]{3,2,1,0:T(8,128)(2,1)} %bitcast.53), calls=%async_computation | async-start | bytes 8388608 | tf_op jit(solution)/shard_map/all_to_all | solution.py:338
  21.5 0.0 reduce-scatter.2.cloned.1.call-start
  21.6 0.8 constant_dynamic-slice_fusion
  22.4 0.1 copy.18
  22.4 0.1 reshape.227
  22.5 0.1 reshape.226
  22.7 1.8 gather_fusion
  24.5 0.1 select_reduce_fusion.3
  24.6 0.1 select_reduce_fusion.2
  24.7 0.1 slice_bitcast_fusion.1
  24.8 1.1 pad_maximum_fusion.wkv_ref
  25.9 0.6 compare_select_fusion.4.entries
  26.5 0.7 compare_convert_fusion.diag_ref
  27.2 1.7 convolution_convert_fusion.2.q_ref
  28.9 1.7 convolution_convert_fusion.1.u_ref
  30.6 2.6 %convert_bitcast_fusion.own_kv_ref = bf16[1024,1024]{1,0:T(8,128)(2,1)} fusion(bf16[1,1024,512]{2,1,0:T(8,128)(2,1)S(1)} %copy-done.2, bf16[512,512]{1,0:T(8,128)(2,1)S(1)} %get-tuple-element.22, bf16[512,512]{1,0:T(8,128)(2,1)S(1)} %get-tuple-element.21), kind=kOutput, calls=%fused_computation.3 | convolution fusion | flops 1076887552 | bytes 4194304 | tf_op jit(solution)/shard_map/dot_general | solution.py:24
  33.2 38.6 %all-to-all-done = bf16[32,2,64,512]{3,2,1,0:T(8,128)(2,1)} async-done(((bf16[32,2,64,512]{3,2,1,0:T(8,128)(2,1)}), bf16[32,2,64,512]{3,2,1,0:T(8,128)(2,1)}, u32[]{:S(2)}, u32[]{:S(2)}) %all-to-all-start) | async-done | bytes 4194336 | tf_op jit(solution)/shard_map/all_to_all | solution.py:338
  71.8 59.9 %shard_map.76 = (bf16[1024,512]{1,0:T(8,128)(2,1)}, bf16[1024,512]{1,0:T(8,128)(2,1)}, bf16[1024,1024]{1,0:T(8,128)(2,1)}, bf16[4096,512]{1,0:T(8,128)(2,1)}, f3...) custom-call(s32[128]{0:T(128)} %compare_select_fusion.4.entries, s32[128]{0:T(128)} %gather_fusion, ...), custom_call_target="tpu_custom_call" | custom-call | tf_op jit(solution)/shard_map/pallas_call | solution.py:196
  131.7 5.6 %collective-permute-start = (f32[2,512,512]{2,1,0:T(8,128)}, f32[2,512,512]{2,1,0:T(8,128)S(1)}, u32[]{:S(2)}, u32[]{:S(2)}) collective-permute-start(f32[2,512,512]{2,1,0:T(8,128)} %get-tuple-element.14), channel_id=1, source_target_pairs={{1,0},{3,2},{5,4},{7,6},{9,8},{11,10},{13,12},{15,14},{17,16},{19,... | collective-permute-start | bytes 6291464 | tf_op jit(solution)/shard_map/ppermute | solution.py:280
  137.3 1.3 collective-permute-start.1
  138.6 2.5 %collective-permute-done = f32[2,512,512]{2,1,0:T(8,128)S(1)} collective-permute-done((f32[2,512,512]{2,1,0:T(8,128)}, f32[2,512,512]{2,1,0:T(8,128)S(1)}, u32[]{:S(2)}, u32[]{:S(2)}) %collective-permute-start) | collective-permute-done | bytes 2097184 | tf_op jit(solution)/shard_map/ppermute | solution.py:280
  141.2 2.6 %collective-permute-done.1 = f32[2,512,512]{2,1,0:T(8,128)} collective-permute-done((f32[2,512,512]{2,1,0:T(8,128)}, f32[2,512,512]{2,1,0:T(8,128)}, u32[]{:S(2)}, u32[]{:S(2)}) %collective-permute-start.1) | collective-permute-done | bytes 2097184 | tf_op jit(solution)/shard_map/ppermute | solution.py:281
  143.7 5.2 %add_select_fusion = f32[2,512,512]{2,1,0:T(8,128)} fusion(f32[2,512,512]{2,1,0:T(8,128)} %get-tuple-element.15, f32[2,512,512]{2,1,0:T(8,128)} %collective-permute-done.1, f32[2,512,512]{2,1,0:T(8,128)} %get-tuple-element.14, f32[2,512,512]{2,1,0:T(8,128)S(1)} %collective-permute-done, pred[]{:T(512)S(6)} %eq.63), kind=kLoop, calls=%fused_computation.2 | loop fusion | flops 1572864 | bytes 10485761 | tf_op jit(solution)/shard_map/jit(_where)/select_n | solution.py:282
  149.0 55.6 %all_to_all.20 = bf16[32,2,64,512]{3,2,1,0:T(8,128)(2,1)} all-to-all(bf16[32,2,64,512]{3,2,1,0:T(8,128)(2,1)} %bitcast.54), channel_id=1, replica_groups=mesh['dp'=4,'verts'=32] {'verts'}, dimensions={0} | all-to-all | bytes 8388608 | tf_op jit(solution)/shard_map/all_to_all | solution.py:353
  204.6 1.8 convert_element_type.41
  206.3 3.6 %all-to-all-start.2 = ((bf16[16,16,512]{2,1,0:T(8,128)(2,1)}), bf16[16,16,512]{2,1,0:T(8,128)(2,1)S(1)}, u32[]{:S(2)}, u32[]{:S(2)}) async-start(bf16[16,16,512]{2,1,0:T(8,128)(2,1)} %bitcast.19), calls=%async_computation.3 | async-start | bytes 524288 | tf_op jit(solution)/shard_map/all_to_all | solution.py:289
  209.9 0.1 reshape.231.send_ref
  210.0 7.4 %all-to-all-done.2 = bf16[16,16,512]{2,1,0:T(8,128)(2,1)S(1)} async-done(((bf16[16,16,512]{2,1,0:T(8,128)(2,1)}), bf16[16,16,512]{2,1,0:T(8,128)(2,1)S(1)}, u32[]{:S(2)}, u32[]{:S(2)}) %all-to-all-start.2) | async-done | bytes 262176 | tf_op jit(solution)/shard_map/all_to_all | solution.py:289
  217.5 0.7 broadcast_in_dim.50
  218.3 3.7 %all-to-all-start.3 = ((bf16[16,16,512]{2,1,0:T(8,128)(2,1)}), bf16[16,16,512]{2,1,0:T(8,128)(2,1)S(1)}, u32[]{:S(2)}, u32[]{:S(2)}) async-start(bf16[16,16,512]{2,1,0:T(8,128)(2,1)} %broadcast_in_dim.50), calls=%async_computation.4 | async-start | bytes 524288 | tf_op jit(solution)/shard_map/all_to_all | solution.py:298
  222.0 2.9 %fusion.20 = f32[1024,512]{1,0:T(8,128)S(1)} fusion(bf16[1024,1024]{1,0:T(8,128)(2,1)} %get-tuple-element.13, bf16[512,512]{1,0:T(8,128)(2,1)S(1)} %get-tuple-element.22, bf16[512,512]{1,0:T(8,128)(2,1)S(1)} %get-tuple-element.21), kind=kOutput, calls=%fused_computation.68 | convolution fusion | flops 1075838976 | bytes 5242880 | tf_op jit(solution)/shard_map/dot_general | solution.py:28
  224.9 4.4 %all-to-all-done.3 = bf16[16,16,512]{2,1,0:T(8,128)(2,1)S(1)} async-done(((bf16[16,16,512]{2,1,0:T(8,128)(2,1)}), bf16[16,16,512]{2,1,0:T(8,128)(2,1)S(1)}, u32[]{:S(2)}, u32[]{:S(2)}) %all-to-all-start.3) | async-done | bytes 262176 | tf_op jit(solution)/shard_map/all_to_all | solution.py:298
  229.3 3.2 %collective-permute-start.2 = (bf16[2,128,512]{2,1,0:T(8,128)(2,1)S(1)}, bf16[2,128,512]{2,1,0:T(8,128)(2,1)S(1)}, u32[]{:S(2)}, u32[]{:S(2)}) collective-permute-start(bf16[2,128,512]{2,1,0:T(8,128)(2,1)S(1)} %bitcast.56), channel_id=1, source_target_pairs={{0,1},{2,3},{4,5},{6,7},{8,9},{10,11},{12,13},{14,15},{16,17},{18,... | collective-permute-start | bytes 786440 | tf_op jit(solution)/shard_map/ppermute | solution.py:306
  232.5 2.3 convolution_add_fusion
  234.8 2.7 %fusion = bf16[1,1024,512]{2,1,0:T(8,128)(2,1)} fusion(bf16[1024,512]{1,0:T(8,128)(2,1)S(1)} %copy-done.5, bf16[4,512,512]{2,1,0:T(8,128)(2,1)} %param.6), kind=kOutput, calls=%fused_computation.8 | convolution fusion | flops 537395200 | bytes 2621440 | tf_op jit(solution)/shard_map/dot_general | solution.py:24
  237.6 2.6 %shard_map.77 = bf16[16,64,512]{2,1,0:T(8,128)(2,1)} custom-call(s32[64]{0:T(128)S(1)} %reshape.231.send_ref, f32[16,64,512]{2,1,0:T(8,128)S(1)} %bitcast.50, bf16[64,64,512]{2,1,0:T(8,128)(2,1)S(1)} %bitcast.49), custom_call_target="tpu_custom_call" | custom-call | tf_op jit(solution)/shard_map/pallas_call | solution.py:259
  240.2 0.1 select_convert_fusion
  240.3 1.0 pad_maximum_fusion.1
  (28 shorter events, 0.2 us)
Async XLA Ops:
  7.2 15.4 %copy-start = (s32[512,64]{0,1:T(8,128)S(1)}, s32[512,64]{0,1:T(8,128)}, u32[]{:S(2)}) copy-start(s32[512,64]{0,1:T(8,128)} %param.9) | copy-start | bytes 393220
  12.8 11.9 %copy-start.3 = (bf16[4,512,512]{2,1,0:T(8,128)(2,1)S(1)}, bf16[4,512,512]{2,1,0:T(8,128)(2,1)}, u32[]{:S(2)}) copy-start(bf16[4,512,512]{2,1,0:T(8,128)(2,1)} %param.6) | copy-start | bytes 6291460
  12.8 59.0 %all-to-all-start = ((bf16[32,2,64,512]{3,2,1,0:T(8,128)(2,1)}), bf16[32,2,64,512]{3,2,1,0:T(8,128)(2,1)}, u32[]{:S(2)}, u32[]{:S(2)}) async-start(bf16[32,2,64,512]{3,2,1,0:T(8,128)(2,1)} %bitcast.53), calls=%async_computation | async-start | bytes 8388608 | tf_op jit(solution)/shard_map/all_to_all | solution.py:338
  21.5 183.0 %reduce-scatter.2.cloned.1.call-start = ((), (), s32[]{:S(2)}) async-start(), calls=%async_computation.5 | async-start | bytes 2621440 | tf_op jit(solution)/shard_map/reduce_scatter | solution.py:283
  24.7 2.5 %copy-start.2 = (bf16[1,1024,512]{2,1,0:T(8,128)(2,1)S(1)}, bf16[1,1024,512]{2,1,0:T(8,128)(2,1)}, u32[]{:S(2)}) copy-start(bf16[1,1024,512]{2,1,0:T(8,128)(2,1)} %param.5) | copy-start | bytes 3145732
  24.8 4.1 %copy-start.4 = (bf16[1,1024,512]{2,1,0:T(8,128)(2,1)S(1)}, bf16[1,1024,512]{2,1,0:T(8,128)(2,1)}, u32[]{:S(2)}) copy-start(bf16[1,1024,512]{2,1,0:T(8,128)(2,1)} %param.7) | copy-start | bytes 3145732
  131.7 9.4 %collective-permute-start = (f32[2,512,512]{2,1,0:T(8,128)}, f32[2,512,512]{2,1,0:T(8,128)S(1)}, u32[]{:S(2)}, u32[]{:S(2)}) collective-permute-start(f32[2,512,512]{2,1,0:T(8,128)} %get-tuple-element.14), channel_id=1, source_target_pairs={{1,0},{3,2},{5,4},{7,6},{9,8},{11,10},{13,12},{15,14},{17,16},{19,... | collective-permute-start | bytes 6291464 | tf_op jit(solution)/shard_map/ppermute | solution.py:280
  137.3 6.4 %collective-permute-start.1 = (f32[2,512,512]{2,1,0:T(8,128)}, f32[2,512,512]{2,1,0:T(8,128)}, u32[]{:S(2)}, u32[]{:S(2)}) collective-permute-start(f32[2,512,512]{2,1,0:T(8,128)} %get-tuple-element.15), channel_id=1, source_target_pairs={{0,1},{2,3},{4,5},{6,7},{8,9},{10,11},{12,13},{14,15},{16,17},{18,... | collective-permute-start | bytes 6291464 | tf_op jit(solution)/shard_map/ppermute | solution.py:281
  206.3 11.1 %all-to-all-start.2 = ((bf16[16,16,512]{2,1,0:T(8,128)(2,1)}), bf16[16,16,512]{2,1,0:T(8,128)(2,1)S(1)}, u32[]{:S(2)}, u32[]{:S(2)}) async-start(bf16[16,16,512]{2,1,0:T(8,128)(2,1)} %bitcast.19), calls=%async_computation.3 | async-start | bytes 524288 | tf_op jit(solution)/shard_map/all_to_all | solution.py:289
  218.3 11.0 %all-to-all-start.3 = ((bf16[16,16,512]{2,1,0:T(8,128)(2,1)}), bf16[16,16,512]{2,1,0:T(8,128)(2,1)S(1)}, u32[]{:S(2)}, u32[]{:S(2)}) async-start(bf16[16,16,512]{2,1,0:T(8,128)(2,1)} %broadcast_in_dim.50), calls=%async_computation.4 | async-start | bytes 524288 | tf_op jit(solution)/shard_map/all_to_all | solution.py:298
  229.3 10.9 %collective-permute-start.2 = (bf16[2,128,512]{2,1,0:T(8,128)(2,1)S(1)}, bf16[2,128,512]{2,1,0:T(8,128)(2,1)S(1)}, u32[]{:S(2)}, u32[]{:S(2)}) collective-permute-start(bf16[2,128,512]{2,1,0:T(8,128)(2,1)S(1)} %bitcast.56), channel_id=1, source_target_pairs={{0,1},{2,3},{4,5},{6,7},{8,9},{10,11},{12,13},{14,15},{16,17},{18,... | collective-permute-start | bytes 786440 | tf_op jit(solution)/shard_map/ppermute | solution.py:306
  232.5 2.3 copy-start.5
  232.5 5.0 %copy-start.1 = (bf16[32,2,64,512]{3,2,1,0:T(8,128)(2,1)S(1)}, bf16[32,2,64,512]{3,2,1,0:T(8,128)(2,1)}, u32[]{:S(2)}) copy-start(bf16[32,2,64,512]{3,2,1,0:T(8,128)(2,1)} %all_to_all.20) | copy-start | bytes 12582916
Sparse Core Ops, SparseCore 0:
  149.1 27.2 reduce-scatter.1

commit v3 on v1

v3 whole, which is shorter than its diff:
```python
import functools
import math

import jax
import jax.numpy as jnp
from jax import lax
from jax.experimental import pallas as pl
from jax.experimental.pallas import tpu as pltpu
from jax.sharding import PartitionSpec as P

H = 8
BS = 64
NNB = 8
CAP = 2

ROWS = 1024
PAIR = 4
HALF = 256

NT = (((1,), (1,)), ((), ()))
TN = (((0,), (0,)), ((), ()))


def dot(a, b):
    return jnp.dot(a, b, preferred_element_type=jnp.float32)


def dot_nt(a, b):
    return lax.dot_general(a, b, NT, preferred_element_type=jnp.float32)


def dot_tn(a, b):
    return lax.dot_general(a, b, TN, preferred_element_type=jnp.float32)


def layer_kernel(
    steps_a,
    steps_b,
    remote,
    scaling,
    entries,
    counts,
    far_ref,
    own_kv_ref,
    wkv_ref,
    q_ref,
    u_ref,
    diag_ref,
    att_ref,
    gq_ref,
    far_grad_ref,
    own_grad_ref,
    back_ref,
    keys,
    values,
    gkeys,
    gvalues,
):
    step = pl.program_id(0)
    per = ROWS // BS
    own = own_kv_ref.shape[0] // BS
    dim = q_ref.shape[1]

    @pl.when(step == 0)
    def _():
        for b in range(own):
            rows = slice(b * BS, (b + 1) * BS)
            keys[remote + b] = own_kv_ref[rows, :dim]
            values[remote + b] = own_kv_ref[rows, dim:]
            gkeys[remote + b] = jnp.zeros((BS, dim), jnp.float32)
            gvalues[remote + b] = jnp.zeros((BS, dim), jnp.float32)

    @pl.when(step < steps_a)
    def _():
        first = pl.ds(step * per, per)
        both = dot(far_ref[...].reshape(ROWS, dim), wkv_ref[...]).astype(jnp.bfloat16)
        keys[first] = both[:, :dim].reshape(per, BS, dim)
        values[first] = both[:, dim:].reshape(per, BS, dim)
        gkeys[first] = jnp.zeros((per, BS, dim), jnp.float32)
        gvalues[first] = jnp.zeros((per, BS, dim), jnp.float32)

    @pl.when((step >= steps_a) & (step < steps_a + steps_b))
    def _():
        place = lax.broadcasted_iota(jnp.int32, (BS, HALF), 0)
        lane_head = lax.broadcasted_iota(jnp.int32, (BS, HALF), 1) // BS
        diag = diag_ref[...]

        def first_half(sub, half):
            at = slice(sub * BS, (sub + 1) * BS)
            cols = slice(half * HALF, (half + 1) * HALF)
            base = ((step - steps_a) * PAIR + sub) * NNB
            ids = [entries[base + n] for n in range(NNB)]
            ends = [counts[base + n] for n in range(NNB)]
            queries = q_ref[at, cols] * jnp.bfloat16(scaling)
            qbd = jnp.concatenate([queries] * (HALF // BS), axis=0) * diag
            ubd = jnp.concatenate([u_ref[at, cols]] * (HALF // BS), axis=0) * diag
            k_all = jnp.concatenate([keys[i, :, cols] for i in ids], axis=0)
            v_all = jnp.concatenate([values[i, :, cols] for i in ids], axis=0)
            return at, cols, ids, ends, qbd, ubd, k_all, v_all, dot_nt(k_all, qbd), dot_nt(v_all, ubd)

        def second_half(at, cols, ids, ends, qbd, ubd, k_all, v_all, scores, dprob):
            scores = jnp.concatenate(
                [
                    jnp.where(place < ends[n], scores[n * BS : (n + 1) * BS], -1e30)
                    for n in range(NNB)
                ],
                axis=0,
            )
            top = jnp.max(scores, axis=0, keepdims=True)
            raised = jnp.exp(scores - top)
            probs = raised * (1.0 / jnp.sum(raised, axis=0, keepdims=True))
            probs_b = probs.astype(jnp.bfloat16)
            inner = jnp.sum(probs * dprob, axis=0, keepdims=True)
            dscore = (probs * (dprob - inner)).astype(jnp.bfloat16)
            grad_v = dot(probs_b, ubd)
            grad_k = dot(dscore, qbd)
            att_wide = dot_tn(probs_b, v_all)
            gq_wide = dot_tn(dscore, k_all)
            att = att_wide[:BS]
            gq = gq_wide[:BS]
            for h in range(1, HALF // BS):
                rows = slice(h * BS, (h + 1) * BS)
                att = jnp.where(lane_head == h, att_wide[rows], att)
                gq = jnp.where(lane_head == h, gq_wide[rows], gq)
            att_ref[at, cols] = att.astype(jnp.bfloat16)
            gq_ref[at, cols] = (gq * scaling).astype(jnp.bfloat16)
            for n in range(NNB):
                rows = slice(n * BS, (n + 1) * BS)
                gkeys[ids[n], :, cols] += grad_k[rows]
                gvalues[ids[n], :, cols] += grad_v[rows]

        todo = [(sub, half) for sub in range(PAIR) for half in range(dim // HALF)]
        held = first_half(*todo[0])
        for after in todo[1:] + [None]:
            ahead = first_half(*after) if after else None
            second_half(*held)
            held = ahead

    @pl.when(step >= steps_a + steps_b)
    def _():
        chunk = step - steps_a - steps_b
        first = pl.ds(chunk * per, per)
        grad_k = gkeys[first].reshape(ROWS, dim).astype(jnp.bfloat16)
        grad_v = gvalues[first].reshape(ROWS, dim).astype(jnp.bfloat16)

        @pl.when(chunk < steps_a)
        def _():
            far_grad_ref[:, :dim] = grad_k
            far_grad_ref[:, dim:] = grad_v
            back = dot_nt(grad_k, wkv_ref[:, :dim]) + dot_nt(grad_v, wkv_ref[:, dim:])
            back_ref[...] = back.astype(jnp.bfloat16).reshape(per, BS, dim)

        @pl.when(chunk >= steps_a)
        def _():
            own_grad_ref[:, :dim] = grad_k
            own_grad_ref[:, dim:] = grad_v


def layer_call(entries, counts, far, own_kv, wkv, queries, ups, scaling):
    parts, _, _, dim = far.shape
    far_rows = parts * CAP * BS
    rows = queries.shape[0]
    blocks = rows // BS
    steps_a = far_rows // ROWS
    steps_c = (far_rows + rows) // ROWS
    steps_b = blocks // PAIR
    table = (far_rows + rows) // BS
    half = steps_a // CAP
    per = ROWS // BS
    head = jnp.arange(HALF, dtype=jnp.int32) // BS
    diag = (head[:, None] == head[None, :]).astype(jnp.bfloat16)

    def at_far(i, *_):
        chunk = jnp.minimum(i, steps_a - 1)
        return (chunk % half, chunk // half, 0, 0)

    def at_b(i, *_):
        return (jnp.clip(i - steps_a, 0, steps_b - 1), 0)

    def at_far_grad(i, *_):
        return (jnp.clip(i - steps_a - steps_b, 0, steps_a - 1), 0)

    def at_own(i, *_):
        return (jnp.maximum(i - 2 * steps_a - steps_b, 0), 0)

    def at_back(i, *_):
        chunk = jnp.clip(i - steps_a - steps_b, 0, steps_a - 1)
        return (chunk % half, chunk // half, 0, 0)

    def whole(shape):
        return pl.BlockSpec(shape, lambda i, *_: (0,) * len(shape), pipeline_mode=pl.Buffered(1))

    return pl.pallas_call(
        functools.partial(layer_kernel, steps_a, steps_b, far_rows // BS, scaling),
        grid_spec=pltpu.PrefetchScalarGridSpec(
            num_scalar_prefetch=2,
            grid=(steps_a + steps_b + steps_c,),
            in_specs=[
                pl.BlockSpec((per, None, BS, dim), at_far),
                whole((rows, 2 * dim)),
                whole((dim, 2 * dim)),
                pl.BlockSpec((PAIR * BS, dim), at_b),
                pl.BlockSpec((PAIR * BS, dim), at_b),
                whole((HALF, HALF)),
            ],
            out_specs=[
                pl.BlockSpec((PAIR * BS, dim), at_b),
                pl.BlockSpec((PAIR * BS, dim), at_b),
                pl.BlockSpec((ROWS, 2 * dim), at_far_grad),
                pl.BlockSpec((ROWS, 2 * dim), at_own),
                pl.BlockSpec((per, None, BS, dim), at_back),
            ],
            scratch_shapes=[
                pltpu.VMEM((table, BS, dim), jnp.bfloat16),
                pltpu.VMEM((table, BS, dim), jnp.bfloat16),
                pltpu.VMEM((table, BS, dim), jnp.float32),
                pltpu.VMEM((table, BS, dim), jnp.float32),
            ],
        ),
        out_shape=[
            jax.ShapeDtypeStruct((rows, dim), jnp.bfloat16),
            jax.ShapeDtypeStruct((rows, dim), jnp.bfloat16),
            jax.ShapeDtypeStruct((far_rows, 2 * dim), jnp.bfloat16),
            jax.ShapeDtypeStruct((rows, 2 * dim), jnp.bfloat16),
            jax.ShapeDtypeStruct((parts, CAP, BS, dim), jnp.bfloat16),
        ],
        compiler_params=pltpu.CompilerParams(vmem_limit_bytes=60 * 2**20),
    )(entries, counts, far, own_kv, wkv, queries, ups, diag)


def weights_kernel(
    steps_far, core, far_ref, far_grad_ref, own_ref, own_grad_ref, gq_ref, att_ref, cot_ref, mine_ref, give_ref, terms
):
    step = pl.program_id(0)
    rows, dim = own_ref.shape

    @pl.when(step == 0)
    def _():
        own = own_ref[...]
        terms[0] = dot_tn(own, gq_ref[...])
        terms[1] = dot_tn(att_ref[...], cot_ref[...])
        terms[2] = dot_tn(own, own_grad_ref[:, :dim])
        terms[3] = dot_tn(own, own_grad_ref[:, dim:])

    @pl.when(step > 0)
    def _():
        far = far_ref[...].reshape(ROWS, dim)
        terms[2] += dot_tn(far, far_grad_ref[:, :dim])
        terms[3] += dot_tn(far, far_grad_ref[:, dim:])

    @pl.when(step == steps_far)
    def _():
        mine_ref[...] = terms[pl.ds(2 * core[0], 2)]
        give_ref[...] = terms[pl.ds(2 - 2 * core[0], 2)].astype(jnp.bfloat16)


def weights_call(core, far, far_grad, own, own_grad, grad_q, attended, cot):
    rows, dim = own.shape
    steps_far = far_grad.shape[0] // ROWS
    half = steps_far // CAP
    per = ROWS // BS

    def at_far(i, *_):
        chunk = jnp.maximum(i - 1, 0)
        return (chunk % half, chunk // half, 0, 0)

    def whole(shape):
        return pl.BlockSpec(shape, lambda i, *_: (0,) * len(shape), pipeline_mode=pl.Buffered(1))

    return pl.pallas_call(
        functools.partial(weights_kernel, steps_far),
        grid_spec=pltpu.PrefetchScalarGridSpec(
            num_scalar_prefetch=1,
            grid=(steps_far + 1,),
            in_specs=[
                pl.BlockSpec((per, None, BS, dim), at_far),
                pl.BlockSpec((ROWS, 2 * dim), lambda i, *_: (jnp.maximum(i - 1, 0), 0)),
                whole((rows, dim)),
                whole((rows, 2 * dim)),
                whole((rows, dim)),
                whole((rows, dim)),
                whole((rows, dim)),
            ],
            out_specs=[whole((2, dim, dim)), whole((2, dim, dim))],
            scratch_shapes=[pltpu.VMEM((4, dim, dim), jnp.float32)],
        ),
        out_shape=[
            jax.ShapeDtypeStruct((2, dim, dim), jnp.float32),
            jax.ShapeDtypeStruct((2, dim, dim), jnp.bfloat16),
        ],
        compiler_params=pltpu.CompilerParams(vmem_limit_bytes=40 * 2**20),
        cost_estimate=pl.CostEstimate(flops=11 * 10**9, bytes_accessed=20 * 10**6, transcendentals=0),
    )(core, far, far_grad, own, own_grad, grad_q, attended, cot)


def combine_kernel(per, send_ref, base_ref, returned_ref, out_ref, acc):
    step = pl.program_id(0)

    @pl.when(step == 0)
    def _():
        acc[...] = base_ref[...]

    for i in range(per):
        for c in range(CAP):
            acc[send_ref[c, step * per + i]] += returned_ref[i, c].astype(jnp.float32)

    @pl.when(step == pl.num_programs(0) - 1)
    def _():
        out_ref[...] = acc[...].astype(jnp.bfloat16)


def combine_call(send, base, returned):
    blocks, _, dim = base.shape
    parts = returned.shape[0]
    per = 8
    return pl.pallas_call(
        functools.partial(combine_kernel, per),
        grid_spec=pltpu.PrefetchScalarGridSpec(
            num_scalar_prefetch=1,
            grid=(parts // per,),
            in_specs=[
                pl.BlockSpec((blocks, BS, dim), lambda i, *_: (0, 0, 0)),
                pl.BlockSpec((per, CAP, BS, dim), lambda i, *_: (i, 0, 0, 0)),
            ],
            out_specs=pl.BlockSpec((blocks, BS, dim), lambda i, *_: (0, 0, 0)),
            scratch_shapes=[pltpu.VMEM((blocks, BS, dim), jnp.float32)],
        ),
        out_shape=jax.ShapeDtypeStruct((blocks, BS, dim), jnp.bfloat16),
        compiler_params=pltpu.CompilerParams(vmem_limit_bytes=32 * 2**20),
    )(send, base, returned)


def sum_weights(mine, give, nparts, me, returned):
    swap = [(v, v ^ 1) for v in range(nparts)]
    half = mine + lax.ppermute(give, "verts", swap).astype(jnp.float32)
    planes = lax.axis_size("dp")
    here = lax.axis_index("dp")
    rows = half.shape[1] // planes
    total = lax.dynamic_slice_in_dim(half, here * rows, rows, 1)
    for d in range(1, planes):
        there = lax.dynamic_slice_in_dim(half, (here + d) % planes * rows, rows, 1)
        move = [(z, (z + d) % planes) for z in range(planes)]
        total += lax.ppermute(there.astype(jnp.bfloat16), "dp", move).astype(jnp.float32)
    half, returned = lax.optimization_barrier((total, returned))
    side = math.isqrt(nparts // 2)
    wide = nparts // side

    def moved(x, y):
        return [
            (v, y(v // wide) * wide + x(v % wide // 2) * 2 + v % 2) for v in range(nparts)
        ]

    def stay(i):
        return i

    def near(i):
        return i ^ 1

    def wrap(i):
        return side - 1 - i

    in_x = [moved(near, stay), moved(wrap, stay)]
    in_y = [moved(stay, near), moved(stay, wrap)]
    one, two = half[0].astype(jnp.bfloat16), half[1].astype(jnp.bfloat16)
    for here, there in zip(in_x + in_y, in_y + in_x):
        one_other = lax.ppermute(one, "verts", here)
        two_other = lax.ppermute(two, "verts", there)
        last = here is in_y[1]
        one = one.astype(jnp.float32) + one_other.astype(jnp.float32)
        two = two.astype(jnp.float32) + two_other.astype(jnp.float32)
        if not last:
            one, two = one.astype(jnp.bfloat16), two.astype(jnp.bfloat16)
    half = jnp.stack([one, two])
    other = lax.ppermute(half, "verts", swap)
    first = me % 2 == 0
    q_o = jnp.where(first, half, other)
    k_v = jnp.where(first, other, half)
    return jnp.concatenate([q_o[:1], k_v, q_o[1:]], axis=0), returned


def local(feats, weights, grad_out, neighbours, valid):
    nparts = lax.axis_size("verts")
    me = lax.axis_index("verts")
    _, rows, dim = feats.shape
    blocks = rows // BS
    scaling = 1.0 / math.sqrt(dim // H)
    part_ids = jnp.arange(nparts, dtype=jnp.int32)
    inputs_now = feats[0]
    cotangent = grad_out[0]
    w_kv = jnp.concatenate([weights[1], weights[2]], axis=1)

    theirs = neighbours.reshape(nparts, blocks * NNB)
    mine = (theirs // blocks == me) & (part_ids[:, None] != me)
    place = theirs % blocks
    low = jnp.min(jnp.where(mine, place, blocks), axis=1)
    high = jnp.max(jnp.where(mine, place, -1), axis=1)
    send = jnp.stack([low % blocks, jnp.maximum(high, 0)])

    lists = lax.dynamic_slice_in_dim(neighbours, me * blocks, blocks, 0).reshape(-1)
    owner = lists // blocks
    named = owner[:, None] == part_ids[None, :]
    lower = jnp.min(jnp.where(named, (lists % blocks)[:, None], blocks), axis=0)
    slot = (jnp.sum(jnp.where(named, lower[None, :], 0), axis=1) != lists % blocks).astype(jnp.int32)
    entries = jnp.where(owner == me, nparts * CAP + lists % blocks, slot * nparts + owner)
    counts = jnp.sum(valid, axis=1)[lists]

    far = lax.all_to_all(
        inputs_now.reshape(blocks, BS, dim)[send.T.reshape(-1)].reshape(nparts, CAP, BS, dim),
        "verts",
        split_axis=0,
        concat_axis=0,
        tiled=True,
    )

    queries = dot(inputs_now, weights[0]).astype(jnp.bfloat16)
    ups = dot_nt(cotangent, weights[3]).astype(jnp.bfloat16)
    own_kv = dot(inputs_now, w_kv).astype(jnp.bfloat16)

    attended, grad_q, far_grad, own_grad, back = layer_call(
        entries, counts, far, own_kv, w_kv, queries, ups, scaling
    )
    returned = lax.all_to_all(back, "verts", split_axis=0, concat_axis=0, tiled=True)
    mine, give = weights_call(
        (me % 2).reshape(1), far, far_grad, inputs_now, own_grad, grad_q, attended, cotangent
    )
    grad_weights, returned = sum_weights(mine, give, nparts, me, returned)

    attn_out = dot(attended, weights[3]).astype(jnp.bfloat16)
    base = dot_nt(grad_q, weights[0]) + dot_nt(own_grad, w_kv)
    grad_feats = combine_call(send, base.reshape(blocks, BS, dim), returned)
    return (attn_out[None], grad_feats.reshape(1, rows, dim), grad_weights)


def solution(mesh):
    in_specs = (P("dp", "verts", None), P(), P("dp", "verts", None), P(), P())
    out_specs = (P("dp", "verts", None), P("dp", "verts", None), P(None, "dp", None))
    return jax.shard_map(local, mesh=mesh, in_specs=in_specs, out_specs=out_specs, check_vma=False)
```

time: 322 us -> 207 us (0.64)
  waiting for transfers between devices: 186 us -> 73.7 us
  starting transfers between devices: 17 us -> 36.5 us
  matrix products: 26.9 us -> 9.73 us
  between operations: 14 us -> 0.96 us
  local copies, waits for them, and re-layouts: 13.3 us -> 17 us
    reduce_scatter x2 -> x0, waiting for transfers between devices: 117 us -> none  [the longest x1 77.1 us: local(): pieces = lax.psum_scatter(flat, 'verts', scatter_dimension=0, tiled=True)]
    all_gather x1 -> x0, waiting for transfers between devices: 32.2 us -> none  [local(): lax.all_gather(pieces, 'verts', axis=0, tiled=True).reshape(shared.shape)]
    ppermute x0 -> x13, waiting for transfers between devices: none -> 27.3 us  [the longest x3 11.3 us: sum_weights(): lax.ppermute(there.astype(jnp.bfloat16), 'dp', move).astype(jnp.float32)]
    ppermute x0 -> x13, starting transfers between devices: none -> 19.7 us  [the longest x4 7.9 us: sum_weights(): one_other = lax.ppermute(one, 'verts', here)]
    dot_general x4 -> x0, matrix products: 13.5 us -> none  [dot_tn(): return lax.dot_general(a, b, TN, preferred_element_type=jnp.float32)]
    pallas_call x0 -> x1, Pallas kernels: none -> 12 us  [weights_call(): pl.pallas_call(functools.partial(weights_kernel, steps_far), grid_spec=pl...]
    all_to_all x2, waiting for transfers between devices: 37.3 us -> 46.4 us  [the longest x1 37.2 us: local(): lax.all_to_all(inputs_now.reshape(blocks, BS, dim)[send.T.reshape(-1)].re...]
    pallas_call x1, Pallas kernels: 51 us -> 43.2 us  [layer_call(): pl.pallas_call(functools.partial(layer_kernel, steps_a, steps_b, far_rows...]
  transfers between devices with their start and end apart: 5 -> 15, of which waited for: 4 -> 13; matrix products, arithmetic and copies ran while one was open for 7% -> 9% of each run, Pallas kernels for 2% -> 8%
where the time goes in v3:
time: 207 us; the launch traced here: 206 us
  waiting for transfers between devices  73.7 us (36%)
  Pallas kernels  60.2 us (29%)
  starting transfers between devices  36.5 us (18%)
  local copies, waits for them, and re-layouts  17 us (8%)
  matrix products  9.73 us (5%)
  other arithmetic  7.93 us (4%)
    pallas_call x1, Pallas kernels, layer_call(): pl.pallas_call(functools.partial(layer_kernel, steps_a, steps_b, far_rows...  43.2 us
    all_to_all x1, waiting for transfers between devices, local(): lax.all_to_all(inputs_now.reshape(blocks, BS, dim)[send.T.reshape(-1)].re...  37.2 us
    pallas_call x1, Pallas kernels, weights_call(): pl.pallas_call(functools.partial(weights_kernel, steps_far), grid_spec=pl...  12 us
    ppermute x3, waiting for transfers between devices, sum_weights(): lax.ppermute(there.astype(jnp.bfloat16), 'dp', move).astype(jnp.float32)  11.3 us
    ppermute x4, waiting for transfers between devices, sum_weights(): two_other = lax.ppermute(two, 'verts', there)  10.1 us
    all_to_all x1, waiting for transfers between devices, local(): lax.all_to_all(back, 'verts', split_axis=0, concat_axis=0, tiled=True)  9.26 us
    all_to_all x1, starting transfers between devices, local(): lax.all_to_all(inputs_now.reshape(blocks, BS, dim)[send.T.reshape(-1)].re...  8.64 us
    all_to_all x1, starting transfers between devices, local(): lax.all_to_all(back, 'verts', split_axis=0, concat_axis=0, tiled=True)  8.15 us
  transfers between devices with their start and end apart: 15, of which 13 were waited for; matrix products, arithmetic and copies ran while one was open for 9% of the time, Pallas kernels for 8%

profile of v3, /device:TPU:1, one launch (start us, length us, event | category | flops | bytes accessed | tf_op | source)
XLA Modules:
  0.0 206.0 jit_solution(15442764702961384194)
XLA Ops:
  0.8 0.8 select_reduce_fusion.1
  2.3 4.0 %gather_fusion.1 = bf16[64,64,512]{2,1,0:T(8,128)(2,1)} fusion(bf16[16,64,512]{2,1,0:T(8,128)(2,1)} %bitcast.56, s32[1024]{0:T(1024)S(1)} %pad_clamp_fusion), kind=kCustom, calls=%fused_computation.1 | custom fusion | bytes 8388864 | tf_op jit(solution)/shard_map/gather | solution.py:408
  6.2 8.6 %all-to-all-start = ((bf16[32,2,64,512]{3,2,1,0:T(8,128)(2,1)}), bf16[32,2,64,512]{3,2,1,0:T(8,128)(2,1)}, u32[]{:S(2)}, u32[]{:S(2)}) async-start(bf16[32,2,64,512]{3,2,1,0:T(8,128)(2,1)} %bitcast.60), calls=%async_computation | async-start | bytes 8388608 | tf_op jit(solution)/shard_map/all_to_all | solution.py:407
  14.9 0.8 constant_dynamic-slice_fusion
  16.0 1.8 gather_fusion
  18.0 1.4 slice_bitcast_fusion.1
  19.4 1.1 pad_maximum_fusion.wkv_ref
  21.2 0.8 compare_convert_fusion.diag_ref
  21.9 1.7 convolution_convert_fusion.2.q_ref
  23.6 1.7 convolution_convert_fusion.1.u_ref
  25.3 2.6 %convert_bitcast_fusion.own_kv_ref = bf16[1024,1024]{1,0:T(8,128)(2,1)} fusion(bf16[1,1024,512]{2,1,0:T(8,128)(2,1)S(1)} %copy-done.1, bf16[512,512]{1,0:T(8,128)(2,1)S(1)} %get-tuple-element.27, bf16[512,512]{1,0:T(8,128)(2,1)S(1)} %get-tuple-element.26), kind=kOutput, calls=%fused_computation.3 | convolution fusion | flops 1076887552 | bytes 4194304 | tf_op jit(solution)/shard_map/dot_general | solution.py:25
  28.0 37.2 %all-to-all-done.far_ref = bf16[32,2,64,512]{3,2,1,0:T(8,128)(2,1)} async-done(((bf16[32,2,64,512]{3,2,1,0:T(8,128)(2,1)}), bf16[32,2,64,512]{3,2,1,0:T(8,128)(2,1)}, u32[]{:S(2)}, u32[]{:S(2)}) %all-to-all-start) | async-done | bytes 4194336 | tf_op jit(solution)/shard_map/all_to_all | solution.py:407
  65.2 43.2 %shard_map.76 = (bf16[1024,512]{1,0:T(8,128)(2,1)}, bf16[1024,512]{1,0:T(8,128)(2,1)}, bf16[4096,1024]{1,0:T(8,128)(2,1)}, bf16[1024,1024]{1,0:T(8,128)(2,1)}, bf16[32,2,64,512]{3,2,1,0:T(8,128)(2,1)}) custom-call(s32[128]{0:T(128)} %compare_select_fusion.5.entries, s32[128]{0:T(128)} %gather_fusion, bf16[32,2,64,512]{3,2,1,0:T(8,128)(2,1)} %all-to-all-done.far_ref, ...), custom_call_target="tpu_custom_call" | custom-call | tf_op jit(solution)/shard_map/pallas_call | solution.py:193
  108.4 8.1 %all-to-all-start.1 = ((bf16[32,2,64,512]{3,2,1,0:T(8,128)(2,1)}), bf16[32,2,64,512]{3,2,1,0:T(8,128)(2,1)}, u32[]{:S(2)}, u32[]{:S(2)}) async-start(bf16[32,2,64,512]{3,2,1,0:T(8,128)(2,1)} %get-tuple-element.18), calls=%async_computation.1 | async-start | bytes 8388608 | tf_op jit(solution)/shard_map/all_to_all | solution.py:422
  116.5 1.2 copy-done.2
  117.8 1.6 copy-done.4
  119.3 1.2 copy-done.7
  120.6 1.2 copy-done.8
  121.8 12.0 %shard_map.77 = (f32[2,512,512]{2,1,0:T(8,128)S(1)}, bf16[2,512,512]{2,1,0:T(8,128)(2,1)}) custom-call(s32[1]{0:T(128)} %bitcast.16.core, bf16[32,2,64,512]{3,2,1,0:T(8,128)(2,1)} %all-to-all-done.far_ref, bf16[4096,1024]{1,0:T(8,128)(2,1)} %get-tuple-element.15.far_grad_ref, bf16[1024,512]{1,0:T(8,128)(2,1)S(1)} %bitcast.57, ...), custom_call_target="tpu_custom_call" | custom-call | flops 11000000512 | bytes 20000000 | tf_op jit(solution)/shard_map/pallas_call | solution.py:270
  134.2 2.5 %collective-permute-done = bf16[2,512,512]{2,1,0:T(8,128)(2,1)S(1)} collective-permute-done((bf16[2,512,512]{2,1,0:T(8,128)(2,1)}, bf16[2,512,512]{2,1,0:T(8,128)(2,1)S(1)}, u32[]{:S(2)}, u32[]{:S(2)}) %collective-permute-start) | collective-permute-done | bytes 1048608 | tf_op jit(solution)/shard_map/ppermute | solution.py:335
  137.0 1.3 copy-done.10
  138.4 0.9 dynamic-slice_convert_fusion.2
  139.3 1.6 collective-permute-start.1
  140.9 3.3 %collective-permute-start.2 = (bf16[2,128,512]{2,1,0:T(8,128)(2,1)}, bf16[2,128,512]{2,1,0:T(8,128)(2,1)}, u32[]{:S(2)}, u32[]{:S(2)}) collective-permute-start(bf16[2,128,512]{2,1,0:T(8,128)(2,1)} %get-tuple-element.25), channel_id=1, source_target_pairs={{0,64},{32,96},{64,0},{96,32},{1,65},{33,97},{65,1},{97,33},{2,66}... | collective-permute-start | bytes 786440 | tf_op jit(solution)/shard_map/ppermute | solution.py:343
  144.2 0.7 collective-permute-start.3
  145.0 4.8 %collective-permute-done.1 = bf16[2,128,512]{2,1,0:T(8,128)(2,1)} collective-permute-done((bf16[2,128,512]{2,1,0:T(8,128)(2,1)}, bf16[2,128,512]{2,1,0:T(8,128)(2,1)}, u32[]{:S(2)}, u32[]{:S(2)}) %collective-permute-start.1) | collective-permute-done | bytes 262176 | tf_op jit(solution)/shard_map/ppermute | solution.py:343
  149.7 6.5 %collective-permute-done.2 = bf16[2,128,512]{2,1,0:T(8,128)(2,1)} collective-permute-done((bf16[2,128,512]{2,1,0:T(8,128)(2,1)}, bf16[2,128,512]{2,1,0:T(8,128)(2,1)}, u32[]{:S(2)}, u32[]{:S(2)}) %collective-permute-start.2) | collective-permute-done | bytes 262176 | tf_op jit(solution)/shard_map/ppermute | solution.py:343
  156.2 1.4 convert_add_fusion.1
  157.6 9.3 %all-to-all-done.1.returned_ref = bf16[32,2,64,512]{3,2,1,0:T(8,128)(2,1)} async-done(((bf16[32,2,64,512]{3,2,1,0:T(8,128)(2,1)}), bf16[32,2,64,512]{3,2,1,0:T(8,128)(2,1)}, u32[]{:S(2)}, u32[]{:S(2)}) %all-to-all-start.1) | async-done | bytes 4194336 | tf_op jit(solution)/shard_map/all_to_all | solution.py:422
  167.6 1.8 collective-permute-start.4
  169.4 1.3 collective-permute-start.8
  170.7 1.4 collective-permute-done.4
  172.1 1.7 collective-permute-done.8
  173.8 1.0 add_convert_fusion.5
  174.9 2.5 %collective-permute-start.5 = (bf16[128,512]{1,0:T(8,128)(2,1)S(1)}, bf16[128,512]{1,0:T(8,128)(2,1)S(1)}, u32[]{:S(2)}, u32[]{:S(2)}) collective-permute-start(bf16[128,512]{1,0:T(8,128)(2,1)S(1)} %get-tuple-element.32), channel_id=1, source_target_pairs={{0,6},{1,7},{2,4},{3,5},{4,2},{5,3},{6,0},{7,1},{8,14},{9,15},{10,... | collective-permute-start | bytes 393224 | tf_op jit(solution)/shard_map/ppermute | solution.py:366
  177.4 1.3 fusion.21
  178.7 1.0 collective-permute-start.9
  180.2 2.1 %collective-permute-start.6 = (bf16[128,512]{1,0:T(8,128)(2,1)S(1)}, bf16[128,512]{1,0:T(8,128)(2,1)S(1)}, u32[]{:S(2)}, u32[]{:S(2)}) collective-permute-start(bf16[128,512]{1,0:T(8,128)(2,1)S(1)} %add_convert_fusion.4), channel_id=1, source_target_pairs={{0,8},{1,9},{2,10},{3,11},{4,12},{5,13},{6,14},{7,15},{8,0},{9,1},... | collective-permute-start | bytes 393224 | tf_op jit(solution)/shard_map/ppermute | solution.py:366
  182.3 2.4 %collective-permute-done.9 = bf16[128,512]{1,0:T(8,128)(2,1)S(1)} collective-permute-done((bf16[128,512]{1,0:T(8,128)(2,1)S(1)}, bf16[128,512]{1,0:T(8,128)(2,1)S(1)}, u32[]{:S(2)}, u32[]{:S(2)}) %collective-permute-start.9) | collective-permute-done | bytes 131104 | tf_op jit(solution)/shard_map/ppermute | solution.py:367
  185.0 1.5 collective-permute-start.7
  186.5 2.1 %collective-permute-done.10 = bf16[128,512]{1,0:T(8,128)(2,1)S(1)} collective-permute-done((bf16[128,512]{1,0:T(8,128)(2,1)S(1)}, bf16[128,512]{1,0:T(8,128)(2,1)S(1)}, u32[]{:S(2)}, u32[]{:S(2)}) %collective-permute-start.10) | collective-permute-done | bytes 131104 | tf_op jit(solution)/shard_map/ppermute | solution.py:367
  188.7 1.4 collective-permute-done.7
  190.1 3.9 %collective-permute-done.11 = bf16[128,512]{1,0:T(8,128)(2,1)S(1)} collective-permute-done((bf16[128,512]{1,0:T(8,128)(2,1)S(1)}, bf16[128,512]{1,0:T(8,128)(2,1)S(1)}, u32[]{:S(2)}, u32[]{:S(2)}) %collective-permute-start.11) | collective-permute-done | bytes 131104 | tf_op jit(solution)/shard_map/ppermute | solution.py:367
  194.1 3.3 %collective-permute-start.12 = (f32[2,128,512]{2,1,0:T(8,128)S(1)}, f32[2,128,512]{2,1,0:T(8,128)S(1)}, u32[]{:S(2)}, u32[]{:S(2)}) collective-permute-start(f32[2,128,512]{2,1,0:T(8,128)S(1)} %pad_maximum_fusion.2), channel_id=1, source_target_pairs={{0,1},{1,0},{2,3},{3,2},{4,5},{5,4},{6,7},{7,6},{8,9},{9,8},{10,11... | collective-permute-start | bytes 1572872 | tf_op jit(solution)/shard_map/ppermute | solution.py:374
  197.4 1.7 fusion
  199.1 0.7 convolution_add_fusion
  199.8 5.0 %shard_map.78 = bf16[16,64,512]{2,1,0:T(8,128)(2,1)} custom-call(s32[2,32]{1,0:T(2,128)S(1)} %get-tuple-element.36.send_ref, f32[16,64,512]{2,1,0:T(8,128)S(1)} %bitcast.58, bf16[32,2,64,512]{3,2,1,0:T(8,128)(2,1)} %all-to-all-done.1.returned_ref), custom_call_target="tpu_custom_call" | custom-call | tf_op jit(solution)/shard_map/pallas_call | solution.py:316
  205.0 1.0 pad_maximum_fusion.1
  (72 shorter events, 4.7 us)
Async XLA Ops:
  0.6 15.3 %copy-start = (s32[512,64]{0,1:T(8,128)S(1)}, s32[512,64]{0,1:T(8,128)}, u32[]{:S(2)}) copy-start(s32[512,64]{0,1:T(8,128)} %param.9) | copy-start | bytes 393220
  6.2 58.9 %all-to-all-start = ((bf16[32,2,64,512]{3,2,1,0:T(8,128)(2,1)}), bf16[32,2,64,512]{3,2,1,0:T(8,128)(2,1)}, u32[]{:S(2)}, u32[]{:S(2)}) async-start(bf16[32,2,64,512]{3,2,1,0:T(8,128)(2,1)} %bitcast.60), calls=%async_computation | async-start | bytes 8388608 | tf_op jit(solution)/shard_map/all_to_all | solution.py:407
  18.0 4.0 %copy-start.1 = (bf16[1,1024,512]{2,1,0:T(8,128)(2,1)S(1)}, bf16[1,1024,512]{2,1,0:T(8,128)(2,1)}, u32[]{:S(2)}) copy-start(bf16[1,1024,512]{2,1,0:T(8,128)(2,1)} %param.5) | copy-start | bytes 3145732
  18.0 4.0 %copy-start.15 = (bf16[4,512,512]{2,1,0:T(8,128)(2,1)S(1)}, bf16[4,512,512]{2,1,0:T(8,128)(2,1)}, u32[]{:S(2)}) copy-start(bf16[4,512,512]{2,1,0:T(8,128)(2,1)} %param.6) | copy-start | bytes 6291460
  19.4 5.9 %copy-start.11 = (bf16[512,512]{1,0:T(8,128)(2,1)}, bf16[512,512]{1,0:T(8,128)(2,1)S(1)}, u32[]{:S(2)}) copy-start(bf16[512,512]{1,0:T(8,128)(2,1)S(1)} %get-tuple-element.26) | copy-start | bytes 1572868
  19.4 5.9 %copy-start.13 = (bf16[512,512]{1,0:T(8,128)(2,1)}, bf16[512,512]{1,0:T(8,128)(2,1)S(1)}, u32[]{:S(2)}) copy-start(bf16[512,512]{1,0:T(8,128)(2,1)S(1)} %get-tuple-element.27) | copy-start | bytes 1572868
  19.4 4.2 %copy-start.6 = (bf16[1,1024,512]{2,1,0:T(8,128)(2,1)S(1)}, bf16[1,1024,512]{2,1,0:T(8,128)(2,1)}, u32[]{:S(2)}) copy-start(bf16[1,1024,512]{2,1,0:T(8,128)(2,1)} %param.7) | copy-start | bytes 3145732
  108.4 58.5 %all-to-all-start.1 = ((bf16[32,2,64,512]{3,2,1,0:T(8,128)(2,1)}), bf16[32,2,64,512]{3,2,1,0:T(8,128)(2,1)}, u32[]{:S(2)}, u32[]{:S(2)}) async-start(bf16[32,2,64,512]{3,2,1,0:T(8,128)(2,1)} %get-tuple-element.18), calls=%async_computation.1 | async-start | bytes 8388608 | tf_op jit(solution)/shard_map/all_to_all | solution.py:422
  116.5 1.2 copy-start.2
  117.8 1.6 copy-start.4
  119.3 1.2 copy-start.7
  120.6 1.2 copy-start.8
  133.8 2.9 %collective-permute-start = (bf16[2,512,512]{2,1,0:T(8,128)(2,1)}, bf16[2,512,512]{2,1,0:T(8,128)(2,1)S(1)}, u32[]{:S(2)}, u32[]{:S(2)}) collective-permute-start(bf16[2,512,512]{2,1,0:T(8,128)(2,1)} %get-tuple-element.17), channel_id=1, source_target_pairs={{0,1},{1,0},{2,3},{3,2},{4,5},{5,4},{6,7},{7,6},{8,9},{9,8},{10,11... | collective-permute-start | bytes 3145736 | tf_op jit(solution)/shard_map/ppermute | solution.py:335
  137.0 1.3 copy-start.10
  138.4 39.0 %copy-start.5 = (bf16[1024,1024]{1,0:T(8,128)(2,1)S(1)}, bf16[1024,1024]{1,0:T(8,128)(2,1)}, u32[]{:S(2)}) copy-start(bf16[1024,1024]{1,0:T(8,128)(2,1)} %get-tuple-element.14.own_grad_ref) | copy-start | bytes 6291460
  138.4 39.0 %copy-start.12 = (bf16[512,512]{1,0:T(8,128)(2,1)S(1)}, bf16[512,512]{1,0:T(8,128)(2,1)}, u32[]{:S(2)}) copy-start(bf16[512,512]{1,0:T(8,128)(2,1)} %copy-done.11) | copy-start | bytes 1572868
  138.4 39.0 %copy-start.14 = (bf16[512,512]{1,0:T(8,128)(2,1)S(1)}, bf16[512,512]{1,0:T(8,128)(2,1)}, u32[]{:S(2)}) copy-start(bf16[512,512]{1,0:T(8,128)(2,1)} %copy-done.13) | copy-start | bytes 1572868
  139.3 10.4 %collective-permute-start.1 = (bf16[2,128,512]{2,1,0:T(8,128)(2,1)}, bf16[2,128,512]{2,1,0:T(8,128)(2,1)}, u32[]{:S(2)}, u32[]{:S(2)}) collective-permute-start(bf16[2,128,512]{2,1,0:T(8,128)(2,1)} %get-tuple-element.23), channel_id=1, source_target_pairs={{0,32},{32,64},{64,96},{96,0},{1,33},{33,65},{65,97},{97,1},{2,34}... | collective-permute-start | bytes 786440 | tf_op jit(solution)/shard_map/ppermute | solution.py:343
  140.9 15.3 %collective-permute-start.2 = (bf16[2,128,512]{2,1,0:T(8,128)(2,1)}, bf16[2,128,512]{2,1,0:T(8,128)(2,1)}, u32[]{:S(2)}, u32[]{:S(2)}) collective-permute-start(bf16[2,128,512]{2,1,0:T(8,128)(2,1)} %get-tuple-element.25), channel_id=1, source_target_pairs={{0,64},{32,96},{64,0},{96,32},{1,65},{33,97},{65,1},{97,33},{2,66}... | collective-permute-start | bytes 786440 | tf_op jit(solution)/shard_map/ppermute | solution.py:343
  144.2 12.0 %collective-permute-start.3 = (bf16[2,128,512]{2,1,0:T(8,128)(2,1)S(1)}, bf16[2,128,512]{2,1,0:T(8,128)(2,1)}, u32[]{:S(2)}, u32[]{:S(2)}) collective-permute-start(bf16[2,128,512]{2,1,0:T(8,128)(2,1)S(1)} %get-tuple-element.24), channel_id=1, source_target_pairs={{0,96},{32,0},{64,32},{96,64},{1,97},{33,1},{65,33},{97,65},{2,98}... | collective-permute-start | bytes 786440 | tf_op jit(solution)/shard_map/ppermute | solution.py:343
  167.6 4.5 %collective-permute-start.4 = (bf16[128,512]{1,0:T(8,128)(2,1)}, bf16[128,512]{1,0:T(8,128)(2,1)}, u32[]{:S(2)}, u32[]{:S(2)}) collective-permute-start(bf16[128,512]{1,0:T(8,128)(2,1)} %get-tuple-element.34), channel_id=1, source_target_pairs={{0,2},{1,3},{2,0},{3,1},{4,6},{5,7},{6,4},{7,5},{8,10},{9,11},{10,... | collective-permute-start | bytes 393224 | tf_op jit(solution)/shard_map/ppermute | solution.py:366
  169.4 4.4 %collective-permute-start.8 = (bf16[128,512]{1,0:T(8,128)(2,1)}, bf16[128,512]{1,0:T(8,128)(2,1)}, u32[]{:S(2)}, u32[]{:S(2)}) collective-permute-start(bf16[128,512]{1,0:T(8,128)(2,1)} %get-tuple-element.35), channel_id=1, source_target_pairs={{0,8},{1,9},{2,10},{3,11},{4,12},{5,13},{6,14},{7,15},{8,0},{9,1},... | collective-permute-start | bytes 393224 | tf_op jit(solution)/shard_map/ppermute | solution.py:367
  174.9 5.3 %collective-permute-start.5 = (bf16[128,512]{1,0:T(8,128)(2,1)S(1)}, bf16[128,512]{1,0:T(8,128)(2,1)S(1)}, u32[]{:S(2)}, u32[]{:S(2)}) collective-permute-start(bf16[128,512]{1,0:T(8,128)(2,1)S(1)} %get-tuple-element.32), channel_id=1, source_target_pairs={{0,6},{1,7},{2,4},{3,5},{4,2},{5,3},{6,0},{7,1},{8,14},{9,15},{10,... | collective-permute-start | bytes 393224 | tf_op jit(solution)/shard_map/ppermute | solution.py:366
  178.6 18.8 %copy-start.9 = (bf16[1024,512]{1,0:T(8,128)(2,1)S(1)}, bf16[1024,512]{1,0:T(8,128)(2,1)}, u32[]{:S(2)}) copy-start(bf16[1024,512]{1,0:T(8,128)(2,1)} %get-tuple-element.12.att_ref) | copy-start | bytes 3145732
  178.6 18.8 %copy-start.16 = (bf16[4,512,512]{2,1,0:T(8,128)(2,1)S(1)}, bf16[4,512,512]{2,1,0:T(8,128)(2,1)}, u32[]{:S(2)}) copy-start(bf16[4,512,512]{2,1,0:T(8,128)(2,1)} %param.6) | copy-start | bytes 6291460
  178.7 6.0 %collective-permute-start.9 = (bf16[128,512]{1,0:T(8,128)(2,1)S(1)}, bf16[128,512]{1,0:T(8,128)(2,1)S(1)}, u32[]{:S(2)}, u32[]{:S(2)}) collective-permute-start(bf16[128,512]{1,0:T(8,128)(2,1)S(1)} %get-tuple-element.33), channel_id=1, source_target_pairs={{0,24},{1,25},{2,26},{3,27},{4,28},{5,29},{6,30},{7,31},{8,16},{9,... | collective-permute-start | bytes 393224 | tf_op jit(solution)/shard_map/ppermute | solution.py:367
  180.2 4.7 %collective-permute-start.6 = (bf16[128,512]{1,0:T(8,128)(2,1)S(1)}, bf16[128,512]{1,0:T(8,128)(2,1)S(1)}, u32[]{:S(2)}, u32[]{:S(2)}) collective-permute-start(bf16[128,512]{1,0:T(8,128)(2,1)S(1)} %add_convert_fusion.4), channel_id=1, source_target_pairs={{0,8},{1,9},{2,10},{3,11},{4,12},{5,13},{6,14},{7,15},{8,0},{9,1},... | collective-permute-start | bytes 393224 | tf_op jit(solution)/shard_map/ppermute | solution.py:366
  184.7 3.9 %collective-permute-start.10 = (bf16[128,512]{1,0:T(8,128)(2,1)S(1)}, bf16[128,512]{1,0:T(8,128)(2,1)S(1)}, u32[]{:S(2)}, u32[]{:S(2)}) collective-permute-start(bf16[128,512]{1,0:T(8,128)(2,1)S(1)} %add_convert_fusion.1), channel_id=1, source_target_pairs={{0,2},{1,3},{2,0},{3,1},{4,6},{5,7},{6,4},{7,5},{8,10},{9,11},{10,... | collective-permute-start | bytes 393224 | tf_op jit(solution)/shard_map/ppermute | solution.py:367
  185.0 5.1 %collective-permute-start.7 = (bf16[128,512]{1,0:T(8,128)(2,1)S(1)}, bf16[128,512]{1,0:T(8,128)(2,1)S(1)}, u32[]{:S(2)}, u32[]{:S(2)}) collective-permute-start(bf16[128,512]{1,0:T(8,128)(2,1)S(1)} %add_convert_fusion.3), channel_id=1, source_target_pairs={{0,24},{1,25},{2,26},{3,27},{4,28},{5,29},{6,30},{7,31},{8,16},{9,... | collective-permute-start | bytes 393224 | tf_op jit(solution)/shard_map/ppermute | solution.py:366
  188.6 5.4 %collective-permute-start.11 = (bf16[128,512]{1,0:T(8,128)(2,1)S(1)}, bf16[128,512]{1,0:T(8,128)(2,1)S(1)}, u32[]{:S(2)}, u32[]{:S(2)}) collective-permute-start(bf16[128,512]{1,0:T(8,128)(2,1)S(1)} %add_convert_fusion), channel_id=1, source_target_pairs={{0,6},{1,7},{2,4},{3,5},{4,2},{5,3},{6,0},{7,1},{8,14},{9,15},{10,... | collective-permute-start | bytes 393224 | tf_op jit(solution)/shard_map/ppermute | solution.py:367
  194.1 5.0 %copy-start.3 = (bf16[1024,512]{1,0:T(8,128)(2,1)S(1)}, bf16[1024,512]{1,0:T(8,128)(2,1)}, u32[]{:S(2)}) copy-start(bf16[1024,512]{1,0:T(8,128)(2,1)} %get-tuple-element.13.gq_ref) | copy-start | bytes 3145732
  194.1 10.7 %collective-permute-start.12 = (f32[2,128,512]{2,1,0:T(8,128)S(1)}, f32[2,128,512]{2,1,0:T(8,128)S(1)}, u32[]{:S(2)}, u32[]{:S(2)}) collective-permute-start(f32[2,128,512]{2,1,0:T(8,128)S(1)} %pad_maximum_fusion.2), channel_id=1, source_target_pairs={{0,1},{1,0},{2,3},{3,2},{4,5},{5,4},{6,7},{7,6},{8,9},{9,8},{10,11... | collective-permute-start | bytes 1572872 | tf_op jit(solution)/shard_map/ppermute | solution.py:374

commit v4 on v3

--- a/solution.py
+++ b/solution.py
@@ -34,61 +34,95 @@
 
 
 def layer_kernel(
-    steps_a,
-    steps_b,
-    remote,
     scaling,
     entries,
     counts,
+    far_hbm,
+    own_k_hbm,
+    own_v_hbm,
+    wkv_hbm,
+    q_hbm,
+    u_hbm,
+    diag_ref,
+    att_hbm,
+    gq_hbm,
+    gk_hbm,
+    gv_hbm,
+    back_hbm,
     far_ref,
-    own_kv_ref,
     wkv_ref,
     q_ref,
     u_ref,
-    diag_ref,
     att_ref,
     gq_ref,
-    far_grad_ref,
-    own_grad_ref,
-    back_ref,
     keys,
     values,
     gkeys,
     gvalues,
+    far_sem,
+    in_sem,
+    out_sem,
+    grad_sem,
 ):
-    step = pl.program_id(0)
+    parts = far_hbm.shape[0]
+    remote = parts * CAP
+    table, _, dim = keys.shape
+    own = table - remote
     per = ROWS // BS
-    own = own_kv_ref.shape[0] // BS
-    dim = q_ref.shape[1]
-
-    @pl.when(step == 0)
-    def _():
-        for b in range(own):
-            rows = slice(b * BS, (b + 1) * BS)
-            keys[remote + b] = own_kv_ref[rows, :dim]
-            values[remote + b] = own_kv_ref[rows, dim:]
-            gkeys[remote + b] = jnp.zeros((BS, dim), jnp.float32)
-            gvalues[remote + b] = jnp.zeros((BS, dim), jnp.float32)
-
-    @pl.when(step < steps_a)
-    def _():
-        first = pl.ds(step * per, per)
-        both = dot(far_ref[...].reshape(ROWS, dim), wkv_ref[...]).astype(jnp.bfloat16)
+    half_parts = parts // per
+    chunks = remote // per
+
+    def far_copy(i):
+        lanes = far_hbm.at[pl.ds(i % half_parts * per, per), i // half_parts]
+        return pltpu.make_async_copy(lanes, far_ref.at[pl.ds(i * per, per)], far_sem.at[i])
+
+    def back_copy(i):
+        lanes = back_hbm.at[pl.ds(i % half_parts * per, per), i // half_parts]
+        return pltpu.make_async_copy(far_ref.at[pl.ds(i * per, per)], lanes, far_sem.at[i])
+
+    def grad_copies(first, count, i):
+        at = pl.ds(first, count)
+        return [
+            pltpu.make_async_copy(keys.at[at], gk_hbm.at[at], grad_sem.at[0, i]),
+            pltpu.make_async_copy(values.at[at], gv_hbm.at[at], grad_sem.at[1, i]),
+        ]
+
+    arrive = [
+        pltpu.make_async_copy(wkv_hbm, wkv_ref, in_sem.at[0]),
+        pltpu.make_async_copy(own_k_hbm, keys.at[pl.ds(remote, own)], in_sem.at[1]),
+        pltpu.make_async_copy(own_v_hbm, values.at[pl.ds(remote, own)], in_sem.at[2]),
+        pltpu.make_async_copy(q_hbm, q_ref, in_sem.at[3]),
+        pltpu.make_async_copy(u_hbm, u_ref, in_sem.at[4]),
+    ]
+    arrive[0].start()
+    for i in range(chunks):
+        far_copy(i).start()
+    for copy in arrive[1:]:
+        copy.start()
+    gkeys[pl.ds(remote, own)] = jnp.zeros((own, BS, dim), jnp.float32)
+    gvalues[pl.ds(remote, own)] = jnp.zeros((own, BS, dim), jnp.float32)
+    arrive[0].wait()
+    for i in range(chunks):
+        first = pl.ds(i * per, per)
+        far_copy(i).wait()
+        both = dot(far_ref[first].reshape(ROWS, dim), wkv_ref[...]).astype(jnp.bfloat16)
         keys[first] = both[:, :dim].reshape(per, BS, dim)
         values[first] = both[:, dim:].reshape(per, BS, dim)
         gkeys[first] = jnp.zeros((per, BS, dim), jnp.float32)
         gvalues[first] = jnp.zeros((per, BS, dim), jnp.float32)
-
-    @pl.when((step >= steps_a) & (step < steps_a + steps_b))
-    def _():
-        place = lax.broadcasted_iota(jnp.int32, (BS, HALF), 0)
-        lane_head = lax.broadcasted_iota(jnp.int32, (BS, HALF), 1) // BS
+    for copy in arrive[1:]:
+        copy.wait()
+
+    place = lax.broadcasted_iota(jnp.int32, (BS, HALF), 0)
+    lane_head = lax.broadcasted_iota(jnp.int32, (BS, HALF), 1) // BS
+
+    def attend(step, carry):
         diag = diag_ref[...]
 
         def first_half(sub, half):
-            at = slice(sub * BS, (sub + 1) * BS)
+            at = pl.ds(pl.multiple_of((step * PAIR + sub) * BS, BS), BS)
             cols = slice(half * HALF, (half + 1) * HALF)
-            base = ((step - steps_a) * PAIR + sub) * NNB
+            base = (step * PAIR + sub) * NNB
             ids = [entries[base + n] for n in range(NNB)]
             ends = [counts[base + n] for n in range(NNB)]
             queries = q_ref[at, cols] * jnp.bfloat16(scaling)
@@ -135,133 +169,126 @@
             ahead = first_half(*after) if after else None
             second_half(*held)
             held = ahead
-
-    @pl.when(step >= steps_a + steps_b)
-    def _():
-        chunk = step - steps_a - steps_b
-        first = pl.ds(chunk * per, per)
-        grad_k = gkeys[first].reshape(ROWS, dim).astype(jnp.bfloat16)
-        grad_v = gvalues[first].reshape(ROWS, dim).astype(jnp.bfloat16)
-
-        @pl.when(chunk < steps_a)
-        def _():
-            far_grad_ref[:, :dim] = grad_k
-            far_grad_ref[:, dim:] = grad_v
-            back = dot_nt(grad_k, wkv_ref[:, :dim]) + dot_nt(grad_v, wkv_ref[:, dim:])
-            back_ref[...] = back.astype(jnp.bfloat16).reshape(per, BS, dim)
-
-        @pl.when(chunk >= steps_a)
-        def _():
-            own_grad_ref[:, :dim] = grad_k
-            own_grad_ref[:, dim:] = grad_v
-
-
-def layer_call(entries, counts, far, own_kv, wkv, queries, ups, scaling):
+        return carry
+
+    lax.fori_loop(0, own // PAIR, attend, 0)
+
+    leave = [
+        pltpu.make_async_copy(att_ref, att_hbm, out_sem.at[0]),
+        pltpu.make_async_copy(gq_ref, gq_hbm, out_sem.at[1]),
+    ]
+    last = pl.ds(remote, own)
+    keys[last] = gkeys[last].astype(jnp.bfloat16)
+    values[last] = gvalues[last].astype(jnp.bfloat16)
+    leave += grad_copies(remote, own, chunks)
+    for copy in leave:
+        copy.start()
+    for i in range(chunks):
+        first = pl.ds(i * per, per)
+        grad_k = gkeys[first].astype(jnp.bfloat16)
+        grad_v = gvalues[first].astype(jnp.bfloat16)
+        keys[first] = grad_k
+        values[first] = grad_v
+        grads = grad_copies(i * per, per, i)
+        for copy in grads:
+            copy.start()
+        back = dot_nt(grad_k.reshape(ROWS, dim), wkv_ref[:, :dim]) + dot_nt(
+            grad_v.reshape(ROWS, dim), wkv_ref[:, dim:]
+        )
+        far_ref[first] = back.astype(jnp.bfloat16).reshape(per, BS, dim)
+        back_copy(i).start()
+        leave += grads + [back_copy(i)]
+    for copy in leave:
+        copy.wait()
+
+
+def layer_call(entries, counts, far, own_k, own_v, wkv, queries, ups, scaling):
     parts, _, _, dim = far.shape
-    far_rows = parts * CAP * BS
     rows = queries.shape[0]
-    blocks = rows // BS
-    steps_a = far_rows // ROWS
-    steps_c = (far_rows + rows) // ROWS
-    steps_b = blocks // PAIR
-    table = (far_rows + rows) // BS
-    half = steps_a // CAP
-    per = ROWS // BS
+    own = rows // BS
+    table = parts * CAP + own
+    chunks = parts * CAP * BS // ROWS
     head = jnp.arange(HALF, dtype=jnp.int32) // BS
     diag = (head[:, None] == head[None, :]).astype(jnp.bfloat16)
-
-    def at_far(i, *_):
-        chunk = jnp.minimum(i, steps_a - 1)
-        return (chunk % half, chunk // half, 0, 0)
-
-    def at_b(i, *_):
-        return (jnp.clip(i - steps_a, 0, steps_b - 1), 0)
-
-    def at_far_grad(i, *_):
-        return (jnp.clip(i - steps_a - steps_b, 0, steps_a - 1), 0)
-
-    def at_own(i, *_):
-        return (jnp.maximum(i - 2 * steps_a - steps_b, 0), 0)
-
-    def at_back(i, *_):
-        chunk = jnp.clip(i - steps_a - steps_b, 0, steps_a - 1)
-        return (chunk % half, chunk // half, 0, 0)
-
-    def whole(shape):
-        return pl.BlockSpec(shape, lambda i, *_: (0,) * len(shape), pipeline_mode=pl.Buffered(1))
-
+    anywhere = pl.BlockSpec(memory_space=pl.ANY)
     return pl.pallas_call(
-        functools.partial(layer_kernel, steps_a, steps_b, far_rows // BS, scaling),
+        functools.partial(layer_kernel, scaling),
         grid_spec=pltpu.PrefetchScalarGridSpec(
             num_scalar_prefetch=2,
-            grid=(steps_a + steps_b + steps_c,),
-            in_specs=[
-                pl.BlockSpec((per, None, BS, dim), at_far),
-                whole((rows, 2 * dim)),
-                whole((dim, 2 * dim)),
-                pl.BlockSpec((PAIR * BS, dim), at_b),
-                pl.BlockSpec((PAIR * BS, dim), at_b),
-                whole((HALF, HALF)),
-            ],
-            out_specs=[
-                pl.BlockSpec((PAIR * BS, dim), at_b),
-                pl.BlockSpec((PAIR * BS, dim), at_b),
-                pl.BlockSpec((ROWS, 2 * dim), at_far_grad),
-                pl.BlockSpec((ROWS, 2 * dim), at_own),
-                pl.BlockSpec((per, None, BS, dim), at_back),
-            ],
+            grid=(1,),
+            in_specs=[anywhere] * 6 + [pl.BlockSpec((HALF, HALF), lambda i, *_: (0, 0))],
+            out_specs=[anywhere] * 5,
             scratch_shapes=[
+                pltpu.VMEM((parts * CAP, BS, dim), jnp.bfloat16),
+                pltpu.VMEM((dim, 2 * dim), jnp.bfloat16),
+                pltpu.VMEM((rows, dim), jnp.bfloat16),
+                pltpu.VMEM((rows, dim), jnp.bfloat16),
+                pltpu.VMEM((rows, dim), jnp.bfloat16),
+                pltpu.VMEM((rows, dim), jnp.bfloat16),
                 pltpu.VMEM((table, BS, dim), jnp.bfloat16),
                 pltpu.VMEM((table, BS, dim), jnp.bfloat16),
                 pltpu.VMEM((table, BS, dim), jnp.float32),
                 pltpu.VMEM((table, BS, dim), jnp.float32),
+                pltpu.SemaphoreType.DMA((chunks,)),
+                pltpu.SemaphoreType.DMA((5,)),
+                pltpu.SemaphoreType.DMA((2,)),
+                pltpu.SemaphoreType.DMA((2, chunks + 1)),
             ],
         ),
         out_shape=[
             jax.ShapeDtypeStruct((rows, dim), jnp.bfloat16),
             jax.ShapeDtypeStruct((rows, dim), jnp.bfloat16),
-            jax.ShapeDtypeStruct((far_rows, 2 * dim), jnp.bfloat16),
-            jax.ShapeDtypeStruct((rows, 2 * dim), jnp.bfloat16),
-            jax.ShapeDtypeStruct((parts, CAP, BS, dim), jnp.bfloat16),
+            jax.ShapeDtypeStruct((table, BS, dim), jnp.bfloat16),
+            jax.ShapeDtypeStruct((table, BS, dim), jnp.bfloat16),
+            jax.ShapeDtypeStruct(far.shape, jnp.bfloat16),
         ],
         compiler_params=pltpu.CompilerParams(vmem_limit_bytes=60 * 2**20),
-    )(entries, counts, far, own_kv, wkv, queries, ups, diag)
+    )(entries, counts, far, own_k, own_v, wkv, queries, ups, diag)
 
 
 def weights_kernel(
-    steps_far, core, far_ref, far_grad_ref, own_ref, own_grad_ref, gq_ref, att_ref, cot_ref, mine_ref, give_ref, terms
+    steps_far, core, far_ref, gk_ref, gv_ref, own_ref, gq_ref, att_ref, cot_ref, mine_ref, give_ref, terms
 ):
     step = pl.program_id(0)
     rows, dim = own_ref.shape
-
-    @pl.when(step == 0)
+    grad_k = gk_ref[...].reshape(ROWS, dim)
+    grad_v = gv_ref[...].reshape(ROWS, dim)
+
+    @pl.when(step < steps_far)
+    def _():
+        far = far_ref[...].reshape(ROWS, dim)
+        from_k = dot_tn(far, grad_k)
+        from_v = dot_tn(far, grad_v)
+
+        @pl.when(step == 0)
+        def _():
+            terms[2] = from_k
+            terms[3] = from_v
+
+        @pl.when(step > 0)
+        def _():
+            terms[2] += from_k
+            terms[3] += from_v
+
+    @pl.when(step == steps_far)
     def _():
         own = own_ref[...]
         terms[0] = dot_tn(own, gq_ref[...])
         terms[1] = dot_tn(att_ref[...], cot_ref[...])
-        terms[2] = dot_tn(own, own_grad_ref[:, :dim])
-        terms[3] = dot_tn(own, own_grad_ref[:, dim:])
-
-    @pl.when(step > 0)
-    def _():
-        far = far_ref[...].reshape(ROWS, dim)
-        terms[2] += dot_tn(far, far_grad_ref[:, :dim])
-        terms[3] += dot_tn(far, far_grad_ref[:, dim:])
-
-    @pl.when(step == steps_far)
-    def _():
+        terms[2] += dot_tn(own, grad_k)
+        terms[3] += dot_tn(own, grad_v)
         mine_ref[...] = terms[pl.ds(2 * core[0], 2)]
         give_ref[...] = terms[pl.ds(2 - 2 * core[0], 2)].astype(jnp.bfloat16)
 
 
-def weights_call(core, far, far_grad, own, own_grad, grad_q, attended, cot):
+def weights_call(core, far, grad_k, grad_v, own, grad_q, attended, cot):
     rows, dim = own.shape
-    steps_far = far_grad.shape[0] // ROWS
+    steps_far = far.shape[0] * CAP * BS // ROWS
     half = steps_far // CAP
     per = ROWS // BS
 
     def at_far(i, *_):
-        chunk = jnp.maximum(i - 1, 0)
+        chunk = jnp.minimum(i, steps_far - 1)
         return (chunk % half, chunk // half, 0, 0)
 
     def whole(shape):
@@ -274,9 +301,9 @@
             grid=(steps_far + 1,),
             in_specs=[
                 pl.BlockSpec((per, None, BS, dim), at_far),
-                pl.BlockSpec((ROWS, 2 * dim), lambda i, *_: (jnp.maximum(i - 1, 0), 0)),
+                pl.BlockSpec((per, BS, dim), lambda i, *_: (i, 0, 0)),
+                pl.BlockSpec((per, BS, dim), lambda i, *_: (i, 0, 0)),
                 whole((rows, dim)),
-                whole((rows, 2 * dim)),
                 whole((rows, dim)),
                 whole((rows, dim)),
                 whole((rows, dim)),
@@ -288,9 +315,9 @@
             jax.ShapeDtypeStruct((2, dim, dim), jnp.float32),
             jax.ShapeDtypeStruct((2, dim, dim), jnp.bfloat16),
         ],
-        compiler_params=pltpu.CompilerParams(vmem_limit_bytes=40 * 2**20),
+        compiler_params=pltpu.CompilerParams(vmem_limit_bytes=60 * 2**20),
         cost_estimate=pl.CostEstimate(flops=11 * 10**9, bytes_accessed=20 * 10**6, transcendentals=0),
-    )(core, far, far_grad, own, own_grad, grad_q, attended, cot)
+    )(core, far, grad_k, grad_v, own, grad_q, attended, cot)
 
 
 def combine_kernel(per, send_ref, base_ref, returned_ref, out_ref, acc):
@@ -341,7 +368,7 @@
         there = lax.dynamic_slice_in_dim(half, (here + d) % planes * rows, rows, 1)
         move = [(z, (z + d) % planes) for z in range(planes)]
         total += lax.ppermute(there.astype(jnp.bfloat16), "dp", move).astype(jnp.float32)
-    half, returned = lax.optimization_barrier((total, returned))
+    half = total
     side = math.isqrt(nparts // 2)
     wide = nparts // side
 
@@ -365,6 +392,8 @@
     for here, there in zip(in_x + in_y, in_y + in_x):
         one_other = lax.ppermute(one, "verts", here)
         two_other = lax.ppermute(two, "verts", there)
+        if here is in_x[0]:
+            one_other, two_other, returned = lax.optimization_barrier((one_other, two_other, returned))
         last = here is in_y[1]
         one = one.astype(jnp.float32) + one_other.astype(jnp.float32)
         two = two.astype(jnp.float32) + two_other.astype(jnp.float32)
@@ -414,19 +443,22 @@
 
     queries = dot(inputs_now, weights[0]).astype(jnp.bfloat16)
     ups = dot_nt(cotangent, weights[3]).astype(jnp.bfloat16)
-    own_kv = dot(inputs_now, w_kv).astype(jnp.bfloat16)
-
-    attended, grad_q, far_grad, own_grad, back = layer_call(
-        entries, counts, far, own_kv, w_kv, queries, ups, scaling
+    own_k = dot(inputs_now, weights[1]).astype(jnp.bfloat16).reshape(blocks, BS, dim)
+    own_v = dot(inputs_now, weights[2]).astype(jnp.bfloat16).reshape(blocks, BS, dim)
+
+    attended, grad_q, grad_k, grad_v, back = layer_call(
+        entries, counts, far, own_k, own_v, w_kv, queries, ups, scaling
     )
     returned = lax.all_to_all(back, "verts", split_axis=0, concat_axis=0, tiled=True)
     mine, give = weights_call(
-        (me % 2).reshape(1), far, far_grad, inputs_now, own_grad, grad_q, attended, cotangent
+        (me % 2).reshape(1), far, grad_k, grad_v, inputs_now, grad_q, attended, cotangent
     )
     grad_weights, returned = sum_weights(mine, give, nparts, me, returned)
 
     attn_out = dot(attended, weights[3]).astype(jnp.bfloat16)
-    base = dot_nt(grad_q, weights[0]) + dot_nt(own_grad, w_kv)
+    own_gk = grad_k[nparts * CAP :].reshape(rows, dim)
+    own_gv = grad_v[nparts * CAP :].reshape(rows, dim)
+    base = dot_nt(grad_q, weights[0]) + dot_nt(own_gk, weights[1]) + dot_nt(own_gv, weights[2])
     grad_feats = combine_call(send, base.reshape(blocks, BS, dim), returned)
     return (attn_out[None], grad_feats.reshape(1, rows, dim), grad_weights)
 

time: 207 us -> 200 us (0.966)
  local copies, waits for them, and re-layouts: 17 us -> 11 us
  waiting for transfers between devices: 73.7 us -> 69.4 us
  matrix products: 9.73 us -> 12.8 us
    all_to_all x1, waiting for transfers between devices: 9.26 us -> 0.01 us  [local(): lax.all_to_all(back, 'verts', split_axis=0, concat_axis=0, tiled=True)]
    unnamed x34 -> x14, local copies, waits for them, and re-layouts: 6.65 us -> 0.04 us
    ppermute x4, waiting for transfers between devices: 3.45 us -> 10 us  [sum_weights(): one_other = lax.ppermute(one, 'verts', here)]
    pallas_call x1, Pallas kernels: 43.2 us -> 39.8 us  [layer_call(): pl.pallas_call(functools.partial(layer_kernel, scaling), grid_spec=pltpu....]
    ppermute x4, starting transfers between devices: 7.9 us -> 5.15 us  [sum_weights(): one_other = lax.ppermute(one, 'verts', here)]
    slice x0 -> x2, local copies, waits for them, and re-layouts: none -> 2.61 us  [the longest x1 1.31 us: local(): own_gk = grad_k[nparts * CAP:].reshape(rows, dim)]
    pallas_call x1, Pallas kernels: 12 us -> 14.6 us  [weights_call(): pl.pallas_call(functools.partial(weights_kernel, steps_far), grid_spec=pl...]
    dot_general x3 -> x4, matrix products: 3.73 us -> 6.09 us  [dot_nt(): return lax.dot_general(a, b, NT, preferred_element_type=jnp.float32)]
  transfers between devices with their start and end apart: 15 -> 15, of which waited for: 13 -> 10; matrix products, arithmetic and copies ran while one was open for 9% -> 13% of each run, Pallas kernels for 8% -> 10%
where the time goes in v4:
time: 200 us; the launch traced here: 199 us
  waiting for transfers between devices  69.4 us (35%)
  Pallas kernels  59.3 us (30%)
  starting transfers between devices  36.3 us (18%)
  matrix products  12.8 us (6%)
  local copies, waits for them, and re-layouts  11 us (6%)
  other arithmetic  9.39 us (5%)
    pallas_call x1, Pallas kernels, layer_call(): pl.pallas_call(functools.partial(layer_kernel, scaling), grid_spec=pltpu....  39.8 us
    all_to_all x1, waiting for transfers between devices, local(): lax.all_to_all(inputs_now.reshape(blocks, BS, dim)[send.T.reshape(-1)].re...  37.8 us
    pallas_call x1, Pallas kernels, weights_call(): pl.pallas_call(functools.partial(weights_kernel, steps_far), grid_spec=pl...  14.6 us
    ppermute x3, waiting for transfers between devices, sum_weights(): lax.ppermute(there.astype(jnp.bfloat16), 'dp', move).astype(jnp.float32)  11.3 us
    ppermute x4, waiting for transfers between devices, sum_weights(): one_other = lax.ppermute(one, 'verts', here)  10 us
    all_to_all x1, starting transfers between devices, local(): lax.all_to_all(inputs_now.reshape(blocks, BS, dim)[send.T.reshape(-1)].re...  8.78 us
    all_to_all x1, starting transfers between devices, local(): lax.all_to_all(back, 'verts', split_axis=0, concat_axis=0, tiled=True)  7.98 us
    ppermute x4, waiting for transfers between devices, sum_weights(): two_other = lax.ppermute(two, 'verts', there)  7.82 us
  transfers between devices with their start and end apart: 15, of which 10 were waited for; matrix products, arithmetic and copies ran while one was open for 13% of the time, Pallas kernels for 10%

profile of v4, /device:TPU:1, one launch (start us, length us, event | category | flops | bytes accessed | tf_op | source)
XLA Modules:
  0.0 199.2 jit_solution(5649403386370698201)
XLA Ops:
  0.8 0.8 select_reduce_fusion.1
  2.3 4.0 %gather_fusion.1 = bf16[64,64,512]{2,1,0:T(8,128)(2,1)} fusion(bf16[16,64,512]{2,1,0:T(8,128)(2,1)} %bitcast.67, s32[1024]{0:T(1024)S(1)} %pad_clamp_fusion), kind=kCustom, calls=%fused_computation.1 | custom fusion | bytes 8388864 | tf_op jit(solution)/shard_map/gather | solution.py:437
  6.2 8.8 %all-to-all-start = ((bf16[32,2,64,512]{3,2,1,0:T(8,128)(2,1)}), bf16[32,2,64,512]{3,2,1,0:T(8,128)(2,1)}, u32[]{:S(2)}, u32[]{:S(2)}) async-start(bf16[32,2,64,512]{3,2,1,0:T(8,128)(2,1)} %bitcast.66), calls=%async_computation | async-start | bytes 8388608 | tf_op jit(solution)/shard_map/all_to_all | solution.py:436
  15.0 0.8 constant_dynamic-slice_fusion
  16.1 1.8 gather_fusion
  18.3 1.1 pad_maximum_fusion.wkv_hbm
  19.4 0.6 compare_select_fusion.5.entries
  19.9 0.8 compare_convert_fusion.diag_ref
  20.7 1.7 convolution_convert_fusion.3
  22.4 1.7 convolution_convert_fusion.4
  24.1 1.7 convolution_convert_fusion.2.q_hbm
  25.7 1.7 convolution_convert_fusion.1.u_hbm
  27.5 37.8 %all-to-all-done.far_hbm.far_ref = bf16[32,2,64,512]{3,2,1,0:T(8,128)(2,1)} async-done(((bf16[32,2,64,512]{3,2,1,0:T(8,128)(2,1)}), bf16[32,2,64,512]{3,2,1,0:T(8,128)(2,1)}, u32[]{:S(2)}, u32[]{:S(2)}) %all-to-all-start) | async-done | bytes 4194336 | tf_op jit(solution)/shard_map/all_to_all | solution.py:436
  65.3 39.8 %shard_map.76 = (bf16[1024,512]{1,0:T(8,128)(2,1)}, bf16[1024,512]{1,0:T(8,128)(2,1)}, bf16[80,64,512]{2,1,0:T(8,128)(2,1)}, bf16[80,64,512]{2,1,0:T(8,128)(2,1)}, bf16[32,2,64,512]{3,2,1,0:T(8,128)(2,1)}) custom-call(s32[128]{0:T(128)} %compare_select_fusion.5.entries, s32[128]{0:T(128)} %gather_fusion, ...), custom_call_target="tpu_custom_call" | custom-call | tf_op jit(solution)/shard_map/pallas_call | solution.py:214
  105.1 8.0 %all-to-all-start.1 = ((bf16[32,2,64,512]{3,2,1,0:T(8,128)(2,1)}), bf16[32,2,64,512]{3,2,1,0:T(8,128)(2,1)}, u32[]{:S(2)}, u32[]{:S(2)}) async-start(bf16[32,2,64,512]{3,2,1,0:T(8,128)(2,1)} %get-tuple-element.19), calls=%async_computation.1 | async-start | bytes 8388608 | tf_op jit(solution)/shard_map/all_to_all | solution.py:452
  113.1 14.6 %shard_map.77 = (f32[2,512,512]{2,1,0:T(8,128)}, bf16[2,512,512]{2,1,0:T(8,128)(2,1)}) custom-call(s32[1]{0:T(128)} %bitcast.19.core, bf16[32,2,64,512]{3,2,1,0:T(8,128)(2,1)} %all-to-all-done.far_hbm.far_ref, bf16[80,64,512]{2,1,0:T(8,128)(2,1)} %get-tuple-element.15.gk_ref, bf16[80,64,512]{2,1,0:T(8,128)(2,1)} %get-tuple-element.16.gv_ref, ...), custom_call_target="tpu_custom_call" | custom-call | flops 11000000512 | bytes 20000000 | tf_op jit(solution)/shard_map/pallas_call | solution.py:297
  127.7 0.6 collective-permute-start
  128.3 2.5 %collective-permute-done = bf16[2,512,512]{2,1,0:T(8,128)(2,1)S(1)} collective-permute-done((bf16[2,512,512]{2,1,0:T(8,128)(2,1)}, bf16[2,512,512]{2,1,0:T(8,128)(2,1)S(1)}, u32[]{:S(2)}, u32[]{:S(2)}) %collective-permute-start) | collective-permute-done | bytes 1048608 | tf_op jit(solution)/shard_map/ppermute | solution.py:362
  130.8 2.0 convert_add_fusion
  132.8 0.9 dynamic-slice_convert_fusion.2
  133.7 1.6 collective-permute-start.1
  135.3 3.3 %collective-permute-start.2 = (bf16[2,128,512]{2,1,0:T(8,128)(2,1)}, bf16[2,128,512]{2,1,0:T(8,128)(2,1)}, u32[]{:S(2)}, u32[]{:S(2)}) collective-permute-start(bf16[2,128,512]{2,1,0:T(8,128)(2,1)} %get-tuple-element.27), channel_id=1, source_target_pairs={{0,64},{32,96},{64,0},{96,32},{1,65},{33,97},{65,1},{97,33},{2,66}... | collective-permute-start | bytes 786440 | tf_op jit(solution)/shard_map/ppermute | solution.py:370
  138.6 0.7 collective-permute-start.3
  139.4 4.8 %collective-permute-done.1 = bf16[2,128,512]{2,1,0:T(8,128)(2,1)} collective-permute-done((bf16[2,128,512]{2,1,0:T(8,128)(2,1)}, bf16[2,128,512]{2,1,0:T(8,128)(2,1)}, u32[]{:S(2)}, u32[]{:S(2)}) %collective-permute-start.1) | collective-permute-done | bytes 262176 | tf_op jit(solution)/shard_map/ppermute | solution.py:370
  144.1 6.5 %collective-permute-done.2 = bf16[2,128,512]{2,1,0:T(8,128)(2,1)} collective-permute-done((bf16[2,128,512]{2,1,0:T(8,128)(2,1)}, bf16[2,128,512]{2,1,0:T(8,128)(2,1)}, u32[]{:S(2)}, u32[]{:S(2)}) %collective-permute-start.2) | collective-permute-done | bytes 262176 | tf_op jit(solution)/shard_map/ppermute | solution.py:370
  150.6 1.3 add_convert_fusion
  151.9 1.2 collective-permute-start.4
  153.1 1.3 collective-permute-start.5
  154.4 1.8 fusion.3
  156.2 1.3 slice.42
  157.5 7.3 %collective-permute-done.4 = bf16[128,512]{1,0:T(8,128)(2,1)} collective-permute-done((bf16[128,512]{1,0:T(8,128)(2,1)S(1)}, bf16[128,512]{1,0:T(8,128)(2,1)}, u32[]{:S(2)}, u32[]{:S(2)}) %collective-permute-start.4) | collective-permute-done | bytes 131104 | tf_op jit(solution)/shard_map/ppermute | solution.py:393
  164.8 1.0 add_convert_fusion.6
  165.9 2.8 %collective-permute-start.6 = (bf16[128,512]{1,0:T(8,128)(2,1)S(1)}, bf16[128,512]{1,0:T(8,128)(2,1)S(1)}, u32[]{:S(2)}, u32[]{:S(2)}) collective-permute-start(bf16[128,512]{1,0:T(8,128)(2,1)S(1)} %get-tuple-element.34), channel_id=1, source_target_pairs={{0,6},{1,7},{2,4},{3,5},{4,2},{5,3},{6,0},{7,1},{8,14},{9,15},{10,... | collective-permute-start | bytes 393224 | tf_op jit(solution)/shard_map/ppermute | solution.py:393
  168.7 1.8 fusion.23
  170.5 2.5 %collective-permute-start.9 = (bf16[128,512]{1,0:T(8,128)(2,1)S(1)}, bf16[128,512]{1,0:T(8,128)(2,1)S(1)}, u32[]{:S(2)}, u32[]{:S(2)}) collective-permute-start(bf16[128,512]{1,0:T(8,128)(2,1)S(1)} %get-tuple-element.35), channel_id=1, source_target_pairs={{0,24},{1,25},{2,26},{3,27},{4,28},{5,29},{6,30},{7,31},{8,16},{9,... | collective-permute-start | bytes 393224 | tf_op jit(solution)/shard_map/ppermute | solution.py:394
  173.2 3.0 %collective-permute-done.9 = bf16[128,512]{1,0:T(8,128)(2,1)S(1)} collective-permute-done((bf16[128,512]{1,0:T(8,128)(2,1)S(1)}, bf16[128,512]{1,0:T(8,128)(2,1)S(1)}, u32[]{:S(2)}, u32[]{:S(2)}) %collective-permute-start.9) | collective-permute-done | bytes 131104 | tf_op jit(solution)/shard_map/ppermute | solution.py:394
  176.3 1.0 collective-permute-done.7
  177.3 1.0 collective-permute-start.8
  178.3 1.8 collective-permute-done.10
  180.2 0.5 collective-permute-start.11
  180.7 1.7 collective-permute-done.8
  182.5 3.0 %collective-permute-done.11 = bf16[128,512]{1,0:T(8,128)(2,1)S(1)} collective-permute-done((bf16[128,512]{1,0:T(8,128)(2,1)S(1)}, bf16[128,512]{1,0:T(8,128)(2,1)S(1)}, u32[]{:S(2)}, u32[]{:S(2)}) %collective-permute-start.11) | collective-permute-done | bytes 131104 | tf_op jit(solution)/shard_map/ppermute | solution.py:394
  185.5 3.7 %collective-permute-start.12 = (f32[2,128,512]{2,1,0:T(8,128)S(1)}, f32[2,128,512]{2,1,0:T(8,128)S(1)}, u32[]{:S(2)}, u32[]{:S(2)}) collective-permute-start(f32[2,128,512]{2,1,0:T(8,128)S(1)} %pad_maximum_fusion.2), channel_id=1, source_target_pairs={{0,1},{1,0},{2,3},{3,2},{4,5},{5,4},{6,7},{7,6},{8,9},{9,8},{10,11... | collective-permute-start | bytes 1572872 | tf_op jit(solution)/shard_map/ppermute | solution.py:403
  189.3 1.7 fusion
  190.9 1.3 slice.43
  192.2 0.8 add_add_fusion
  193.0 5.0 %shard_map.78 = bf16[16,64,512]{2,1,0:T(8,128)(2,1)} custom-call(s32[2,32]{1,0:T(2,128)S(1)} %get-tuple-element.38.send_ref, f32[16,64,512]{2,1,0:T(8,128)S(1)} %bitcast.65, bf16[32,2,64,512]{3,2,1,0:T(8,128)(2,1)} %all-to-all-done.1.returned_ref), custom_call_target="tpu_custom_call" | custom-call | tf_op jit(solution)/shard_map/pallas_call | solution.py:343
  198.2 1.0 pad_maximum_fusion.1
  (56 shorter events, 2.0 us)
Async XLA Ops:
  0.6 15.4 %copy-start = (s32[512,64]{0,1:T(8,128)S(1)}, s32[512,64]{0,1:T(8,128)}, u32[]{:S(2)}) copy-start(s32[512,64]{0,1:T(8,128)} %param.9) | copy-start | bytes 393220
  6.2 11.9 %copy-start.2 = (bf16[4,512,512]{2,1,0:T(8,128)(2,1)S(1)}, bf16[4,512,512]{2,1,0:T(8,128)(2,1)}, u32[]{:S(2)}) copy-start(bf16[4,512,512]{2,1,0:T(8,128)(2,1)} %param.6) | copy-start | bytes 6291460
  6.2 59.0 %all-to-all-start = ((bf16[32,2,64,512]{3,2,1,0:T(8,128)(2,1)}), bf16[32,2,64,512]{3,2,1,0:T(8,128)(2,1)}, u32[]{:S(2)}, u32[]{:S(2)}) async-start(bf16[32,2,64,512]{3,2,1,0:T(8,128)(2,1)} %bitcast.66), calls=%async_computation | async-start | bytes 8388608 | tf_op jit(solution)/shard_map/all_to_all | solution.py:436
  18.2 2.5 %copy-start.1 = (bf16[1,1024,512]{2,1,0:T(8,128)(2,1)S(1)}, bf16[1,1024,512]{2,1,0:T(8,128)(2,1)}, u32[]{:S(2)}) copy-start(bf16[1,1024,512]{2,1,0:T(8,128)(2,1)} %param.5) | copy-start | bytes 3145732
  24.1 1.7 copy-start.5
  105.1 59.8 %all-to-all-start.1 = ((bf16[32,2,64,512]{3,2,1,0:T(8,128)(2,1)}), bf16[32,2,64,512]{3,2,1,0:T(8,128)(2,1)}, u32[]{:S(2)}, u32[]{:S(2)}) async-start(bf16[32,2,64,512]{3,2,1,0:T(8,128)(2,1)} %get-tuple-element.19), calls=%async_computation.1 | async-start | bytes 8388608 | tf_op jit(solution)/shard_map/all_to_all | solution.py:452
  127.7 3.1 %collective-permute-start = (bf16[2,512,512]{2,1,0:T(8,128)(2,1)}, bf16[2,512,512]{2,1,0:T(8,128)(2,1)S(1)}, u32[]{:S(2)}, u32[]{:S(2)}) collective-permute-start(bf16[2,512,512]{2,1,0:T(8,128)(2,1)} %get-tuple-element.18), channel_id=1, source_target_pairs={{0,1},{1,0},{2,3},{3,2},{4,5},{5,4},{6,7},{7,6},{8,9},{9,8},{10,11... | collective-permute-start | bytes 3145736 | tf_op jit(solution)/shard_map/ppermute | solution.py:362
  132.8 21.6 %copy-start.4 = (bf16[1024,512]{1,0:T(8,128)(2,1)S(1)}, bf16[1024,512]{1,0:T(8,128)(2,1)}, u32[]{:S(2)}) copy-start(bf16[1024,512]{1,0:T(8,128)(2,1)} %get-tuple-element.14.gq_ref) | copy-start | bytes 3145732
  133.7 10.4 %collective-permute-start.1 = (bf16[2,128,512]{2,1,0:T(8,128)(2,1)}, bf16[2,128,512]{2,1,0:T(8,128)(2,1)}, u32[]{:S(2)}, u32[]{:S(2)}) collective-permute-start(bf16[2,128,512]{2,1,0:T(8,128)(2,1)} %get-tuple-element.25), channel_id=1, source_target_pairs={{0,32},{32,64},{64,96},{96,0},{1,33},{33,65},{65,97},{97,1},{2,34}... | collective-permute-start | bytes 786440 | tf_op jit(solution)/shard_map/ppermute | solution.py:370
  135.3 15.3 %collective-permute-start.2 = (bf16[2,128,512]{2,1,0:T(8,128)(2,1)}, bf16[2,128,512]{2,1,0:T(8,128)(2,1)}, u32[]{:S(2)}, u32[]{:S(2)}) collective-permute-start(bf16[2,128,512]{2,1,0:T(8,128)(2,1)} %get-tuple-element.27), channel_id=1, source_target_pairs={{0,64},{32,96},{64,0},{96,32},{1,65},{33,97},{65,1},{97,33},{2,66}... | collective-permute-start | bytes 786440 | tf_op jit(solution)/shard_map/ppermute | solution.py:370
  138.6 12.0 %collective-permute-start.3 = (bf16[2,128,512]{2,1,0:T(8,128)(2,1)S(1)}, bf16[2,128,512]{2,1,0:T(8,128)(2,1)}, u32[]{:S(2)}, u32[]{:S(2)}) collective-permute-start(bf16[2,128,512]{2,1,0:T(8,128)(2,1)S(1)} %get-tuple-element.26), channel_id=1, source_target_pairs={{0,96},{32,0},{64,32},{96,64},{1,97},{33,1},{65,33},{97,65},{2,98}... | collective-permute-start | bytes 786440 | tf_op jit(solution)/shard_map/ppermute | solution.py:370
  151.9 12.9 %collective-permute-start.4 = (bf16[128,512]{1,0:T(8,128)(2,1)S(1)}, bf16[128,512]{1,0:T(8,128)(2,1)}, u32[]{:S(2)}, u32[]{:S(2)}) collective-permute-start(bf16[128,512]{1,0:T(8,128)(2,1)S(1)} %get-tuple-element.37), channel_id=1, source_target_pairs={{0,2},{1,3},{2,0},{3,1},{4,6},{5,7},{6,4},{7,5},{8,10},{9,11},{10,... | collective-permute-start | bytes 393224 | tf_op jit(solution)/shard_map/ppermute | solution.py:393
  153.1 11.7 %collective-permute-start.5 = (bf16[128,512]{1,0:T(8,128)(2,1)S(1)}, bf16[128,512]{1,0:T(8,128)(2,1)}, u32[]{:S(2)}, u32[]{:S(2)}) collective-permute-start(bf16[128,512]{1,0:T(8,128)(2,1)S(1)} %get-tuple-element.36), channel_id=1, source_target_pairs={{0,8},{1,9},{2,10},{3,11},{4,12},{5,13},{6,14},{7,15},{8,0},{9,1},... | collective-permute-start | bytes 393224 | tf_op jit(solution)/shard_map/ppermute | solution.py:394
  165.9 7.2 %collective-permute-start.6 = (bf16[128,512]{1,0:T(8,128)(2,1)S(1)}, bf16[128,512]{1,0:T(8,128)(2,1)S(1)}, u32[]{:S(2)}, u32[]{:S(2)}) collective-permute-start(bf16[128,512]{1,0:T(8,128)(2,1)S(1)} %get-tuple-element.34), channel_id=1, source_target_pairs={{0,6},{1,7},{2,4},{3,5},{4,2},{5,3},{6,0},{7,1},{8,14},{9,15},{10,... | collective-permute-start | bytes 393224 | tf_op jit(solution)/shard_map/ppermute | solution.py:393
  170.5 18.8 %copy-start.3 = (bf16[4,512,512]{2,1,0:T(8,128)(2,1)S(1)}, bf16[4,512,512]{2,1,0:T(8,128)(2,1)}, u32[]{:S(2)}) copy-start(bf16[4,512,512]{2,1,0:T(8,128)(2,1)} %param.6) | copy-start | bytes 6291460
  170.5 18.8 %copy-start.6 = (bf16[1024,512]{1,0:T(8,128)(2,1)S(1)}, bf16[1024,512]{1,0:T(8,128)(2,1)}, u32[]{:S(2)}) copy-start(bf16[1024,512]{1,0:T(8,128)(2,1)} %get-tuple-element.13.att_ref) | copy-start | bytes 3145732
  170.5 5.7 %collective-permute-start.9 = (bf16[128,512]{1,0:T(8,128)(2,1)S(1)}, bf16[128,512]{1,0:T(8,128)(2,1)S(1)}, u32[]{:S(2)}, u32[]{:S(2)}) collective-permute-start(bf16[128,512]{1,0:T(8,128)(2,1)S(1)} %get-tuple-element.35), channel_id=1, source_target_pairs={{0,24},{1,25},{2,26},{3,27},{4,28},{5,29},{6,30},{7,31},{8,16},{9,... | collective-permute-start | bytes 393224 | tf_op jit(solution)/shard_map/ppermute | solution.py:394
  173.1 4.2 %collective-permute-start.7 = (bf16[128,512]{1,0:T(8,128)(2,1)S(1)}, bf16[128,512]{1,0:T(8,128)(2,1)S(1)}, u32[]{:S(2)}, u32[]{:S(2)}) collective-permute-start(bf16[128,512]{1,0:T(8,128)(2,1)S(1)} %add_convert_fusion.5), channel_id=1, source_target_pairs={{0,8},{1,9},{2,10},{3,11},{4,12},{5,13},{6,14},{7,15},{8,0},{9,1},... | collective-permute-start | bytes 393224 | tf_op jit(solution)/shard_map/ppermute | solution.py:393
  176.2 3.9 %collective-permute-start.10 = (bf16[128,512]{1,0:T(8,128)(2,1)S(1)}, bf16[128,512]{1,0:T(8,128)(2,1)S(1)}, u32[]{:S(2)}, u32[]{:S(2)}) collective-permute-start(bf16[128,512]{1,0:T(8,128)(2,1)S(1)} %add_convert_fusion.2), channel_id=1, source_target_pairs={{0,2},{1,3},{2,0},{3,1},{4,6},{5,7},{6,4},{7,5},{8,10},{9,11},{10,... | collective-permute-start | bytes 393224 | tf_op jit(solution)/shard_map/ppermute | solution.py:394
  177.3 5.1 %collective-permute-start.8 = (bf16[128,512]{1,0:T(8,128)(2,1)S(1)}, bf16[128,512]{1,0:T(8,128)(2,1)S(1)}, u32[]{:S(2)}, u32[]{:S(2)}) collective-permute-start(bf16[128,512]{1,0:T(8,128)(2,1)S(1)} %add_convert_fusion.4), channel_id=1, source_target_pairs={{0,24},{1,25},{2,26},{3,27},{4,28},{5,29},{6,30},{7,31},{8,16},{9,... | collective-permute-start | bytes 393224 | tf_op jit(solution)/shard_map/ppermute | solution.py:393
  180.2 5.3 %collective-permute-start.11 = (bf16[128,512]{1,0:T(8,128)(2,1)S(1)}, bf16[128,512]{1,0:T(8,128)(2,1)S(1)}, u32[]{:S(2)}, u32[]{:S(2)}) collective-permute-start(bf16[128,512]{1,0:T(8,128)(2,1)S(1)} %add_convert_fusion.1), channel_id=1, source_target_pairs={{0,6},{1,7},{2,4},{3,5},{4,2},{5,3},{6,0},{7,1},{8,14},{9,15},{10,... | collective-permute-start | bytes 393224 | tf_op jit(solution)/shard_map/ppermute | solution.py:394
  185.5 12.5 %collective-permute-start.12 = (f32[2,128,512]{2,1,0:T(8,128)S(1)}, f32[2,128,512]{2,1,0:T(8,128)S(1)}, u32[]{:S(2)}, u32[]{:S(2)}) collective-permute-start(f32[2,128,512]{2,1,0:T(8,128)S(1)} %pad_maximum_fusion.2), channel_id=1, source_target_pairs={{0,1},{1,0},{2,3},{3,2},{4,5},{5,4},{6,7},{7,6},{8,9},{9,8},{10,11... | collective-permute-start | bytes 1572872 | tf_op jit(solution)/shard_map/ppermute | solution.py:403
